TPU v7x, 128 devices: a whole 4x4x4 slice. The times are simulated.
128 devices in a mesh: section: 8 (over z, core), tensor: 16 (over y, x).
Axes of the slice: x: 4, y: 4, z: 4, core: 2. Of those that a mesh axis runs over, the one named last changes fastest.
Arguments:
- attn_logits: bfloat16 [8, 64, 96, 96], P('section', 'tensor'), may hold values from -7.5 to 256
- out_weight: bfloat16 [8, 8192, 5120], P('section', 'tensor'), may hold values from -0.0625 to 0.0625
- value_weight: bfloat16 [8, 1024, 5120], P('section', 'tensor'), may hold values from -0.078125 to 0.078125
- norm_gain: float32 [8, 5120], P('section'), may hold values from 0.1 to 1.9
- norm_scale: float32 [8, 96], P('section', 'tensor'), may hold values from 0.5 to 2
- target_encoder: bfloat16 [16384, 5120], P(None, ('section', 'tensor')), may hold values from -6 to 6
- target_ids: int32 [2], replicated, may hold values from 0 to 16383
- target_token: int32 [2], replicated, may hold values from 48 to 95, as said below
- decoder: bfloat16 [8, 16384, 5120], P('section', 'tensor'), may hold values from -0.078125 to 0.078125
- source_ids: int32 [8, 96, 128], P('section'), may hold values from 0 to 16383, all different within a row
- source_values: float32 [8, 96, 128], P('section'), may hold values from 0.05 to 0.6
Outputs:
- edges: float32 [8, 96, 2, 128], P('section', 'tensor')
Inputs may be any that keep to these rules, and one draw needn't show every extreme that they name: `target_token`: the targets' tokens are distinct, and the last token is always one of them.
All inputs are finite; a program needn't handle non-finite values.
Results may differ from a plain program's by a relative error of at most 0.04.
Values may be sent and summed in bfloat16 or wider, within the bound.
A program may use at most 64 MiB of HBM per device.

v0:
```python
import jax
import jax.numpy as jnp
from jax import lax
from jax.sharding import PartitionSpec as P

KV = 8
HD = 128
TARGETS = 2


def swapped(value, axis, distance):
    mask = 2**distance
    pairs = [(source, source ^ mask) for source in range(lax.axis_size(axis))]
    return lax.ppermute(value, axis, pairs)


def from_behind(array, axis, by):
    peers = lax.axis_size(axis)
    pairs = [(i, i + by) for i in range(peers) if 0 <= i + by < peers]
    return lax.ppermute(array, axis, pairs)


def frozen_pattern(logits):
    scores = logits.astype(jnp.float32)
    query_pos = lax.broadcasted_iota(jnp.int32, scores.shape, scores.ndim - 2)
    key_pos = lax.broadcasted_iota(jnp.int32, scores.shape, scores.ndim - 1)
    scores = jnp.where(key_pos <= query_pos, scores, -jnp.inf)
    highest = jnp.max(scores, axis=-1, keepdims=True)
    weights = jnp.exp(scores - highest)
    return (weights / jnp.sum(weights, axis=-1, keepdims=True)).astype(jnp.bfloat16)


def pull_back(gradient, gathered, pattern, out_rows, value_rows, gain_row, scale_row):
    tok_count, per_micro, model_width = gathered.shape
    head_count = pattern.shape[0]
    head_grad = jnp.einsum("tkd,ed->tke", gathered, out_rows, preferred_element_type=jnp.float32)
    head_grad = head_grad.astype(jnp.bfloat16).reshape(tok_count, per_micro, head_count, HD)
    value_part = jnp.einsum("hts,tkhc->skc", pattern, head_grad, preferred_element_type=jnp.float32)
    sharing = lax.axis_size("tensor") // KV
    shard_index = lax.axis_index("tensor")
    for bit_number in reversed(range(sharing.bit_length() - 1)):
        half_width = value_part.shape[-1] // 2
        split_parts = value_part.reshape(tok_count, per_micro, 2, half_width)
        upper_bit = shard_index >> bit_number & 1
        kept_half = jnp.where(upper_bit == 1, split_parts[:, :, 1], split_parts[:, :, 0])
        sent_half = jnp.where(upper_bit == 1, split_parts[:, :, 0], split_parts[:, :, 1])
        value_part = kept_half + swapped(
            sent_half.astype(jnp.bfloat16), "tensor", bit_number
        ).astype(sent_half.dtype)
    value_grad = value_part.astype(jnp.bfloat16)
    mixed = lax.psum_scatter(
        jnp.einsum(
            "tkw,wd->tkd", value_grad, value_rows, preferred_element_type=jnp.float32
        ).astype(jnp.bfloat16),
        "tensor",
        scatter_dimension=0,
        tiled=True,
    ).astype(jnp.float32)
    change = mixed * gain_row[None, None, :] * scale_row[:, None, None]
    return (gradient.astype(jnp.float32) + change).astype(jnp.bfloat16)


def body(
    attn_logits,
    out_weight,
    value_weight,
    norm_gain,
    norm_scale,
    target_encoder,
    target_ids,
    target_token,
    decoder,
    source_ids,
    source_values,
):
    layers_here = out_weight.shape[0]
    model_width = out_weight.shape[2]
    tok_local = norm_scale.shape[1]
    tok_count = attn_logits.shape[2]
    section_count = lax.axis_size("section")
    section_index = lax.axis_index("section")
    shard_index = lax.axis_index("tensor")
    picked_rows = jnp.take(target_encoder, target_ids, axis=0)
    encoded = lax.all_gather(picked_rows, ("section", "tensor"), axis=1, tiled=True)
    token_global = shard_index * tok_local + jnp.arange(tok_local, dtype=jnp.int32)
    hit = token_global[:, None, None] == target_token[None, :, None]
    seed_slab = jnp.where(hit, encoded[None, :, :], jnp.zeros_like(encoded)[None, :, :])
    patterns = frozen_pattern(attn_logits)
    micro_count = 1
    per_micro = TARGETS // micro_count
    step_total = section_count + micro_count - 1
    is_top = section_index == section_count - 1

    def advance(step_index, carry):
        inbox, kept_slab = carry
        micro_slot = step_index - (section_count - 1 - section_index)
        active = (micro_slot >= 0) & (micro_slot < micro_count)
        micro_slot = jnp.clip(micro_slot, 0, micro_count - 1)
        gradient = jnp.where(is_top, seed_slab, inbox)
        for layer_index in reversed(range(layers_here)):
            gathered = lax.all_gather(gradient, "tensor", axis=0, tiled=True)
            layer_slab = kept_slab[layer_index]
            updated = jnp.where(active, gathered, layer_slab)
            kept_slab = kept_slab.at[layer_index].set(updated)
            gradient = pull_back(
                gradient,
                gathered,
                patterns[layer_index],
                out_weight[layer_index],
                value_weight[layer_index],
                norm_gain[layer_index],
                norm_scale[layer_index],
            )
        inbox = from_behind(gradient, "section", -1)
        return (inbox, kept_slab)

    inbox_start = jnp.zeros((tok_local, per_micro, model_width), jnp.bfloat16)
    kept_start = jnp.zeros((layers_here, tok_count, TARGETS, model_width), jnp.bfloat16)
    inbox_end, kept_slab = lax.fori_loop(0, step_total, advance, (inbox_start, kept_start))
    feat_rows = decoder.shape[1]
    active_count = source_ids.shape[2]
    layer_index = 0
    scores = jnp.einsum(
        "tkd,fd->tkf",
        kept_slab[layer_index],
        decoder[layer_index],
        preferred_element_type=jnp.float32,
    )
    local_source = source_ids[layer_index] - shard_index * feat_rows
    source_mask = (local_source >= 0) & (local_source < feat_rows)
    index_table = jnp.broadcast_to(
        jnp.clip(local_source, 0, feat_rows - 1)[:, None, :], (tok_count, TARGETS, active_count)
    )
    chosen = jnp.take_along_axis(scores, index_table, axis=2)
    weights = jnp.where(source_mask, source_values[layer_index], 0.0)
    edge_list = [chosen * weights[:, None, :]]
    edge_terms = jnp.stack(edge_list, axis=0)
    return lax.psum_scatter(
        edge_terms.astype(jnp.bfloat16), "tensor", scatter_dimension=1, tiled=True
    ).astype(jnp.float32)


def solution(mesh):
    return jax.shard_map(
        body,
        mesh=mesh,
        in_specs=(
            P("section", "tensor", None, None),
            P("section", "tensor", None),
            P("section", "tensor", None),
            P("section", None),
            P("section", "tensor"),
            P(None, ("section", "tensor")),
            P(),
            P(),
            P("section", "tensor", None),
            P("section", None, None),
            P("section", None, None),
        ),
        out_specs=P("section", "tensor", None, None),
        check_vma=False,
    )
```

profile of v0, /device:TPU:0, one launch (start us, length us, event | category | flops | bytes accessed | tf_op | source)
XLA Modules:
  0.0 1639.9 jit_solution(9704272776966137765)
XLA Ops:
  14.1 4.6 copy.35
  22.1 51.3 %all-gather = bf16[128,40,2]{1,2,0:T(2,128)(2,1)S(1)} all-gather(bf16[1,40,2]{1,2,0:T(2,128)(2,1)S(1)} %fusion.33), channel_id=1, replica_groups=mesh['section'=8,'tensor'=16] {'section','tensor'}, dimensions={0}, use_global_device_ids=true | all-gather | bytes 20640 | tf_op jit(solution)/shard_map/all_gather | solution.py:84
  74.7 1243.2 %while.20 = (s32[]{:T(128)}, bf16[6,2,5120]{2,1,0:T(2,128)(2,1)S(1)}, bf16[1,96,2,5120]{3,2,1,0:T(2,128)(2,1)S(1)}, pred[]{:T(512)}, bf16[1,512,5120]{2,1,0:T(8,...) while((s32[]{:T(128)}, ...), condition=%wide.region_4.5_spmd.clone, body=%wide.region_2.4_spmd.clone.sunk | while | flops 1155059712 | bytes 39948804 | solution.py:119
  75.9 44.8 %all-gather.3.cloned.1.call-done = bf16[96,2,5120]{2,1,0:T(2,128)(2,1)} async-done(((bf16[6,2,5120]{2,1,0:T(2,128)(2,1)}), bf16[96,2,5120]{2,1,0:T(2,128)(2,1)}) %all-gather.3.cloned.1.call-update) | async-done | bytes 1966096 | tf_op jit(solution)/shard_map/while/body/eval_jaxpr/all_gather | solution.py:101
  120.7 5.0 fusion.49
  130.7 3.3 copy.62
  135.3 87.3 %all-reduce.6.cloned.1.call-done = bf16[96,2,5120]{2,1,0:T(2,128)(2,1)} async-done(((bf16[96,2,5120]{2,1,0:T(2,128)(2,1)}), bf16[96,2,5120]{2,1,0:T(2,128)(2,1)}) %all-reduce.6.cloned.1.call-update) | async-done | bytes 1966096 | tf_op jit(solution)/shard_map/while
  228.4 48.0 %all-gather.3.cloned.1.call-done = bf16[96,2,5120]{2,1,0:T(2,128)(2,1)} async-done(((bf16[6,2,5120]{2,1,0:T(2,128)(2,1)}), bf16[96,2,5120]{2,1,0:T(2,128)(2,1)}) %all-gather.3.cloned.1.call-update) | async-done | bytes 1966096 | tf_op jit(solution)/shard_map/while/body/eval_jaxpr/all_gather | solution.py:101
  276.4 5.0 fusion.49
  291.0 87.3 %all-reduce.6.cloned.1.call-done = bf16[96,2,5120]{2,1,0:T(2,128)(2,1)} async-done(((bf16[96,2,5120]{2,1,0:T(2,128)(2,1)}), bf16[96,2,5120]{2,1,0:T(2,128)(2,1)}) %all-reduce.6.cloned.1.call-update) | async-done | bytes 1966096 | tf_op jit(solution)/shard_map/while
  384.1 47.6 %all-gather.3.cloned.1.call-done = bf16[96,2,5120]{2,1,0:T(2,128)(2,1)} async-done(((bf16[6,2,5120]{2,1,0:T(2,128)(2,1)}), bf16[96,2,5120]{2,1,0:T(2,128)(2,1)}) %all-gather.3.cloned.1.call-update) | async-done | bytes 1966096 | tf_op jit(solution)/shard_map/while/body/eval_jaxpr/all_gather | solution.py:101
  431.7 5.0 fusion.49
  446.3 87.3 %all-reduce.6.cloned.1.call-done = bf16[96,2,5120]{2,1,0:T(2,128)(2,1)} async-done(((bf16[96,2,5120]{2,1,0:T(2,128)(2,1)}), bf16[96,2,5120]{2,1,0:T(2,128)(2,1)}) %all-reduce.6.cloned.1.call-update) | async-done | bytes 1966096 | tf_op jit(solution)/shard_map/while
  539.4 48.2 %all-gather.3.cloned.1.call-done = bf16[96,2,5120]{2,1,0:T(2,128)(2,1)} async-done(((bf16[6,2,5120]{2,1,0:T(2,128)(2,1)}), bf16[96,2,5120]{2,1,0:T(2,128)(2,1)}) %all-gather.3.cloned.1.call-update) | async-done | bytes 1966096 | tf_op jit(solution)/shard_map/while/body/eval_jaxpr/all_gather | solution.py:101
  587.6 5.0 fusion.49
  602.2 87.3 %all-reduce.6.cloned.1.call-done = bf16[96,2,5120]{2,1,0:T(2,128)(2,1)} async-done(((bf16[96,2,5120]{2,1,0:T(2,128)(2,1)}), bf16[96,2,5120]{2,1,0:T(2,128)(2,1)}) %all-reduce.6.cloned.1.call-update) | async-done | bytes 1966096 | tf_op jit(solution)/shard_map/while
  695.3 48.1 %all-gather.3.cloned.1.call-done = bf16[96,2,5120]{2,1,0:T(2,128)(2,1)} async-done(((bf16[6,2,5120]{2,1,0:T(2,128)(2,1)}), bf16[96,2,5120]{2,1,0:T(2,128)(2,1)}) %all-gather.3.cloned.1.call-update) | async-done | bytes 1966096 | tf_op jit(solution)/shard_map/while/body/eval_jaxpr/all_gather | solution.py:101
  743.4 5.0 fusion.49
  758.0 87.3 %all-reduce.6.cloned.1.call-done = bf16[96,2,5120]{2,1,0:T(2,128)(2,1)} async-done(((bf16[96,2,5120]{2,1,0:T(2,128)(2,1)}), bf16[96,2,5120]{2,1,0:T(2,128)(2,1)}) %all-reduce.6.cloned.1.call-update) | async-done | bytes 1966096 | tf_op jit(solution)/shard_map/while
  851.1 47.8 %all-gather.3.cloned.1.call-done = bf16[96,2,5120]{2,1,0:T(2,128)(2,1)} async-done(((bf16[6,2,5120]{2,1,0:T(2,128)(2,1)}), bf16[96,2,5120]{2,1,0:T(2,128)(2,1)}) %all-gather.3.cloned.1.call-update) | async-done | bytes 1966096 | tf_op jit(solution)/shard_map/while/body/eval_jaxpr/all_gather | solution.py:101
  898.9 5.0 fusion.49
  913.5 87.3 %all-reduce.6.cloned.1.call-done = bf16[96,2,5120]{2,1,0:T(2,128)(2,1)} async-done(((bf16[96,2,5120]{2,1,0:T(2,128)(2,1)}), bf16[96,2,5120]{2,1,0:T(2,128)(2,1)}) %all-reduce.6.cloned.1.call-update) | async-done | bytes 1966096 | tf_op jit(solution)/shard_map/while
  1006.6 47.8 %all-gather.3.cloned.1.call-done = bf16[96,2,5120]{2,1,0:T(2,128)(2,1)} async-done(((bf16[6,2,5120]{2,1,0:T(2,128)(2,1)}), bf16[96,2,5120]{2,1,0:T(2,128)(2,1)}) %all-gather.3.cloned.1.call-update) | async-done | bytes 1966096 | tf_op jit(solution)/shard_map/while/body/eval_jaxpr/all_gather | solution.py:101
  1054.4 5.0 fusion.49
  1069.0 87.3 %all-reduce.6.cloned.1.call-done = bf16[96,2,5120]{2,1,0:T(2,128)(2,1)} async-done(((bf16[96,2,5120]{2,1,0:T(2,128)(2,1)}), bf16[96,2,5120]{2,1,0:T(2,128)(2,1)}) %all-reduce.6.cloned.1.call-update) | async-done | bytes 1966096 | tf_op jit(solution)/shard_map/while
  1162.1 47.5 %all-gather.3.cloned.1.call-done = bf16[96,2,5120]{2,1,0:T(2,128)(2,1)} async-done(((bf16[6,2,5120]{2,1,0:T(2,128)(2,1)}), bf16[96,2,5120]{2,1,0:T(2,128)(2,1)}) %all-gather.3.cloned.1.call-update) | async-done | bytes 1966096 | tf_op jit(solution)/shard_map/while/body/eval_jaxpr/all_gather | solution.py:101
  1209.6 5.0 fusion.49
  1224.3 87.3 %all-reduce.6.cloned.1.call-done = bf16[96,2,5120]{2,1,0:T(2,128)(2,1)} async-done(((bf16[96,2,5120]{2,1,0:T(2,128)(2,1)}), bf16[96,2,5120]{2,1,0:T(2,128)(2,1)}) %all-reduce.6.cloned.1.call-update) | async-done | bytes 1966096 | tf_op jit(solution)/shard_map/while
  1314.1 3.8 fusion.51
  1317.9 7.6 fusion.26
  1325.5 234.6 %gather_fusion.1 = f32[24576]{0:T(1024)S(1)} fusion(f32[96,2,1024]{2,0,1:T(8,128)S(1)} %fusion.26, s32[24576]{0:T(1024)S(1)} %bitcast.117), kind=kCustom, calls=%fused_computation.1 | custom fusion | bytes 491520 | tf_op jit(solution)/shard_map/jit(take_along_axis)/gather | solution.py:134
  1560.2 72.5 %all-reduce.1 = bf16[1,96,2,128]{3,2,1,0:T(2,128)(2,1)S(1)} all-reduce(bf16[1,96,2,128]{3,2,1,0:T(2,128)(2,1)S(1)} %fusion.32), channel_id=3, replica_groups=mesh['section'=8,'tensor'=16] {'tensor'}, use_global_device_ids=true, to_apply=%region_5.6.clone | all-reduce | flops 24576 | bytes 98304
  (174 shorter events, 124.0 us)
Async XLA Ops:
  74.9 45.8 %all-gather.3.cloned.1.call-start = ((), (), s32[]{:S(2)}) async-start(), calls=%async_computation | async-start | bytes 2088960 | tf_op jit(solution)/shard_map/while/body/eval_jaxpr/all_gather | solution.py:101
  75.9 146.8 %all-reduce.6.cloned.1.call-start = ((), (), s32[]{:S(2)}) async-start(), calls=%async_computation.1 | async-start | bytes 3932160 | tf_op jit(solution)/shard_map/while
  126.0 4.0 collective-permute-start
  223.8 3.5 collective-permute-start.1
  227.4 49.0 %all-gather.3.cloned.1.call-start = ((), (), s32[]{:S(2)}) async-start(), calls=%async_computation | async-start | bytes 2088960 | tf_op jit(solution)/shard_map/while/body/eval_jaxpr/all_gather | solution.py:101
  228.3 150.0 %all-reduce.6.cloned.1.call-start = ((), (), s32[]{:S(2)}) async-start(), calls=%async_computation.1 | async-start | bytes 3932160 | tf_op jit(solution)/shard_map/while
  281.7 4.0 collective-permute-start
  379.6 3.5 collective-permute-start.1
  383.1 48.6 %all-gather.3.cloned.1.call-start = ((), (), s32[]{:S(2)}) async-start(), calls=%async_computation | async-start | bytes 2088960 | tf_op jit(solution)/shard_map/while/body/eval_jaxpr/all_gather | solution.py:101
  384.1 149.5 %all-reduce.6.cloned.1.call-start = ((), (), s32[]{:S(2)}) async-start(), calls=%async_computation.1 | async-start | bytes 3932160 | tf_op jit(solution)/shard_map/while
  437.0 4.0 collective-permute-start
  534.8 3.5 collective-permute-start.1
  538.4 49.2 %all-gather.3.cloned.1.call-start = ((), (), s32[]{:S(2)}) async-start(), calls=%async_computation | async-start | bytes 2088960 | tf_op jit(solution)/shard_map/while/body/eval_jaxpr/all_gather | solution.py:101
  539.3 150.2 %all-reduce.6.cloned.1.call-start = ((), (), s32[]{:S(2)}) async-start(), calls=%async_computation.1 | async-start | bytes 3932160 | tf_op jit(solution)/shard_map/while
  592.9 4.0 collective-permute-start
  690.7 3.5 collective-permute-start.1
  694.3 49.1 %all-gather.3.cloned.1.call-start = ((), (), s32[]{:S(2)}) async-start(), calls=%async_computation | async-start | bytes 2088960 | tf_op jit(solution)/shard_map/while/body/eval_jaxpr/all_gather | solution.py:101
  695.2 150.1 %all-reduce.6.cloned.1.call-start = ((), (), s32[]{:S(2)}) async-start(), calls=%async_computation.1 | async-start | bytes 3932160 | tf_op jit(solution)/shard_map/while
  748.7 4.0 collective-permute-start
  846.5 3.5 collective-permute-start.1
  850.1 48.9 %all-gather.3.cloned.1.call-start = ((), (), s32[]{:S(2)}) async-start(), calls=%async_computation | async-start | bytes 2088960 | tf_op jit(solution)/shard_map/while/body/eval_jaxpr/all_gather | solution.py:101
  851.0 149.8 %all-reduce.6.cloned.1.call-start = ((), (), s32[]{:S(2)}) async-start(), calls=%async_computation.1 | async-start | bytes 3932160 | tf_op jit(solution)/shard_map/while
  904.2 4.0 collective-permute-start
  1002.0 3.5 collective-permute-start.1
  1005.6 48.9 %all-gather.3.cloned.1.call-start = ((), (), s32[]{:S(2)}) async-start(), calls=%async_computation | async-start | bytes 2088960 | tf_op jit(solution)/shard_map/while/body/eval_jaxpr/all_gather | solution.py:101
  1006.5 149.8 %all-reduce.6.cloned.1.call-start = ((), (), s32[]{:S(2)}) async-start(), calls=%async_computation.1 | async-start | bytes 3932160 | tf_op jit(solution)/shard_map/while
  1059.8 4.0 collective-permute-start
  1157.6 3.5 collective-permute-start.1
  1161.1 48.5 %all-gather.3.cloned.1.call-start = ((), (), s32[]{:S(2)}) async-start(), calls=%async_computation | async-start | bytes 2088960 | tf_op jit(solution)/shard_map/while/body/eval_jaxpr/all_gather | solution.py:101
  1162.1 149.5 %all-reduce.6.cloned.1.call-start = ((), (), s32[]{:S(2)}) async-start(), calls=%async_computation.1 | async-start | bytes 3932160 | tf_op jit(solution)/shard_map/while
  1215.0 4.0 collective-permute-start
  1312.8 5.1 collective-permute-start.1
  (9 other events, 1070.1 us)
Sparse Core Ops, SparseCore 0:
  77.9 42.7 all-gather.2
  134.2 88.3 all-reduce.5
  230.4 46.0 all-gather.2
  289.9 88.4 all-reduce.5
  385.8 45.8 all-gather.2
  445.2 88.3 all-reduce.5
  541.4 46.2 all-gather.2
  601.1 88.3 all-reduce.5
  697.3 46.0 all-gather.2
  756.9 88.3 all-reduce.5
  853.0 45.8 all-gather.2
  912.4 88.3 all-reduce.5
  1008.6 45.8 all-gather.2
  1067.9 88.3 all-reduce.5
  1163.8 45.8 all-gather.2
  1223.1 88.3 all-reduce.5
where the time goes:
time: 1640 us
  waiting for transfers between devices  1100 us (67%)
  local copies, waits for them, and re-layouts  278 us (17%)
  blocking collectives  124 us (8%)
  matrix products  54.6 us (3%)
  other arithmetic  41.5 us (3%)
  starting transfers between devices  20.9 us (1%)
    while x24, waiting for transfers between devices  699 us
    all_gather x8, waiting for transfers between devices, advance(): gathered = lax.all_gather(gradient, 'tensor', axis=0, tiled=True)  380 us
    gather x1, local copies, waits for them, and re-layouts, body(): chosen = jnp.take_along_axis(scores, index_table, axis=2)  235 us
    unnamed x1, blocking collectives  72.5 us
    all_gather x1, blocking collectives, body(): lax.all_gather(picked_rows, ('section', 'tensor'), axis=1, tiled=True)  51.3 us
    dot_general x8, matrix products, pull_back(): jnp.einsum('tkd,ed->tke', gathered, out_rows, preferred_element_type=jnp....  39.7 us
  transfers between devices with their start and end apart: 32, of which 24 were waited for; matrix products, arithmetic and copies ran while one was open for 1% of the time, Pallas kernels for 0%

commit v1 on v0

v1 whole, which is shorter than its diff:
```python
import jax
import jax.numpy as jnp
from jax import lax
from jax.experimental import pallas as pl
from jax.experimental.pallas import tpu as pltpu
from jax.sharding import PartitionSpec as P

MESH = pl.DeviceIdType.MESH
F32 = jnp.float32
BF16 = jnp.bfloat16

TOK = 96
N = 16
TOP = 7
HD = 128
WIDE = 640
HEADS_HERE = 4
ACT = 128
FEATS = 1024


def nt_dot(a, b):
    return lax.dot_general(a, b, (((1,), (1,)), ((), ())), preferred_element_type=F32)


def chain_kernel(
    enc_ref, scale_ref, logits_ref, gain_ref, tok_ref, ids_ref, vals_ref,
    wo_hbm, wv_hbm, dec_hbm,
    out_ref,
    wo, dec, wvs, grad, grad_send, v_send, v_recv, sc_recv, sc_rows,
    e1_recv, e2_send, e2_recv, pat, hcat, pad, acc, ed_send, ed_recv,
    local_sem, wv_ssem, wv_rsem, sc_ssem, sc_rsem, e1_ssem, e1_rsem, e2_ssem, e2_rsem,
    v_ssem, v_rsem, g_ssem, g_rsem, hop_ssem, ed_ssem, ed_rsem,
):
    s = lax.axis_index("section")
    j = lax.axis_index("tensor")
    my_k = lax.rem(j, 2)
    my_d = j // 2

    def peer(o):
        return lax.rem(j + o, N)

    def remote(src, dst, ssem, rsem, section, index):
        return pltpu.make_async_remote_copy(
            src_ref=src, dst_ref=dst, send_sem=ssem, recv_sem=rsem,
            device_id=(section, index), device_id_type=MESH,
        )

    def arrived(dst, rsem, ssem):
        remote(dst, dst, ssem, rsem, s, peer(1)).wait_recv()

    barrier = pltpu.get_barrier_semaphore()

    def greet(section, index):
        pl.semaphore_signal(barrier, inc=1, device_id=(section, index), device_id_type=MESH)

    @pl.when(s < TOP)
    def _():
        greet(TOP, j)

    @pl.when(s == TOP)
    def _():
        for q in range(TOP):
            greet(q, j)

    @pl.when(s < TOP - 1)
    def _():
        greet(s + 1, j)

    @pl.when((s >= 1) & (s < TOP))
    def _():
        greet(s - 1, j)

    @pl.loop(1, N)
    def _(o):
        greet(s, peer(o))

    wo_copy = pltpu.make_async_copy(wo_hbm, wo, local_sem.at[0])
    wo_copy.start()
    own_cols = pl.ds(pl.multiple_of(my_d * WIDE, 128), WIDE)
    own_rows = pl.ds(pl.multiple_of(j * 64, 64), 64)
    wv_copy = pltpu.make_async_copy(wv_hbm.at[:, own_cols], wvs.at[own_rows], local_sem.at[1])
    wv_copy.start()
    dec_copy = pltpu.make_async_copy(dec_hbm, dec, local_sem.at[2])
    dec_copy.start()

    pl.semaphore_wait(
        barrier,
        15
        + jnp.where(s == TOP, TOP, 1)
        + jnp.where(s < TOP - 1, 1, 0)
        + jnp.where((s >= 1) & (s < TOP), 1, 0),
    )

    @pl.when(s < TOP)
    def _():
        remote(enc_ref, e1_recv.at[s], e1_ssem, e1_rsem.at[s], TOP, j).start()

    def sc_copy(o):
        return remote(scale_ref, sc_recv.at[j], sc_ssem.at[o], sc_rsem.at[j], s, peer(o))

    def wv_peer_copy(o):
        p = peer(o)
        cols = pl.ds(pl.multiple_of((p // 2) * WIDE, 128), WIDE)
        return remote(
            wv_hbm.at[:, cols], wvs.at[own_rows], wv_ssem.at[o], wv_rsem.at[j], s, p
        )

    def start_weights():
        @pl.when(s >= 1)
        def _():
            @pl.loop(1, N)
            def _(o):
                sc_copy(o).start()
                wv_peer_copy(o).start()

    @pl.when(s < TOP)
    def _():
        start_weights()

    pad[...] = jnp.zeros_like(pad)
    hcat[...] = jnp.zeros_like(hcat)
    query = lax.broadcasted_iota(jnp.int32, (TOK, TOK), 0)
    key = lax.broadcasted_iota(jnp.int32, (TOK, TOK), 1)
    for h in range(HEADS_HERE):
        scores = jnp.where(key <= query, logits_ref[h].astype(F32), -jnp.inf)
        highest = jnp.max(scores, axis=-1, keepdims=True)
        weights = jnp.exp(scores - highest)
        pad[0:TOK, 0:TOK] = weights / jnp.sum(weights, axis=-1, keepdims=True)
        pat[:, h * HD : (h + 1) * HD] = pad[...].T[0:TOK, :].astype(BF16)

    @pl.when(s == TOP)
    def _():
        e1_recv[TOP] = enc_ref[...]
        for q in range(TOP):
            arrived(e1_recv.at[q], e1_rsem.at[q], e1_ssem)
        rows = jnp.concatenate([e1_recv[:, 0, :], e1_recv[:, 1, :]], axis=0)
        e2_send[...] = rows.astype(BF16)
        e2_recv[j] = rows.astype(BF16)

        def e2_copy(o):
            return remote(e2_send, e2_recv.at[j], e2_ssem.at[o], e2_rsem.at[j], s, peer(o))

        @pl.loop(1, N)
        def _(o):
            e2_copy(o).start()

        start_weights()

        @pl.loop(1, N)
        def _(o):
            p = peer(o)
            arrived(e2_recv.at[p], e2_rsem.at[p], e2_ssem.at[o])

        blocks = [jnp.zeros((16, 128), F32) for _ in range(5)]
        for q in range(N):
            first = min(40 * q // 128, 3)
            piece = e2_recv[q].astype(F32)
            blocks[first] = blocks[first] + piece[:, 0:128]
            blocks[first + 1] = blocks[first + 1] + piece[:, 128:256]
        top_rows = jnp.concatenate(blocks, axis=1)
        token = lax.broadcasted_iota(jnp.int32, (TOK, WIDE), 0)
        for k in range(2):
            hit = token == tok_ref[k]
            for d in range(8):
                row = jnp.broadcast_to(top_rows[k * 8 + d : k * 8 + d + 1, :], (TOK, WIDE))
                grad[2 * d + k] = jnp.where(hit, row, 0.0).astype(BF16)

        @pl.loop(1, N)
        def _(o):
            e2_copy(o).wait_send()

    def chunk_copy(o):
        return remote(grad.at[j], grad.at[j], g_ssem.at[o], g_rsem.at[j], s, peer(o))

    @pl.when(s < TOP)
    def _():
        arrived(grad.at[j], g_rsem.at[j], g_ssem.at[0])

        @pl.loop(1, N)
        def _(o):
            chunk_copy(o).start()

    wo_copy.wait()
    wv_copy.wait()

    def v_copy(k, d):
        p = 2 * d + k
        return remote(
            v_send.at[k], v_recv.at[j], v_ssem.at[p], v_rsem.at[j], s, p
        )

    def hop_copy():
        return remote(grad_send, grad.at[j], hop_ssem, g_rsem.at[j], s - 1, j)

    def wait_chunk(c):
        @pl.when((s < TOP) & (c != j))
        def _():
            arrived(grad.at[c], g_rsem.at[c], g_ssem.at[0])

    def consume():
        @pl.loop(1, N)
        def _(o):
            p = peer(o)
            arrived(v_recv.at[p], v_rsem.at[p], v_ssem.at[0])

        pieces = []
        for q in range(8):
            both = v_recv[2 * q].astype(F32) + v_recv[2 * q + 1].astype(F32)
            pieces.append((both * sc_rows[...]).astype(BF16))
        value_grad = jnp.concatenate(pieces, axis=1)
        mixed = jnp.dot(value_grad, wvs[...], preferred_element_type=F32)
        grad_send[...] = (grad[j].astype(F32) + mixed * gain_ref[:, own_cols]).astype(BF16)
        hop_copy().start()

    @pl.when(s >= 1)
    def _():
        @pl.loop(1, N)
        def _(o):
            p = peer(o)
            arrived(sc_recv.at[p], sc_rsem.at[p], sc_ssem.at[0])
            rows = pl.ds(pl.multiple_of(p * 64, 64), 64)
            arrived(wvs.at[rows], wv_rsem.at[p], wv_ssem.at[0])

        sc_recv[j] = scale_ref[...]
        for q in range(N):
            sc_rows[6 * q : 6 * q + 6, :] = sc_recv[q, 0:6, :]

        @pl.loop(0, 2)
        def _(k):
            total = jnp.zeros((TOK, HEADS_HERE * HD), F32)
            for d in range(8):
                wait_chunk(2 * d + k)
                total += nt_dot(grad[2 * d + k], wo[:, d * WIDE : (d + 1) * WIDE])
            head_grad = total.astype(BF16)
            for h in range(HEADS_HERE):
                hcat[h * HD : h * HD + TOK, :] = head_grad[:, h * HD : (h + 1) * HD]
            part = jnp.dot(pat[...], hcat[...], preferred_element_type=F32).astype(BF16)
            v_send[k] = part
            for d in range(8):
                @pl.when(2 * d + k != j)
                def _():
                    v_copy(k, d).start()

            @pl.when(my_k == k)
            def _():
                v_recv[j] = part
                consume()

    @pl.when(s == 0)
    def _():
        for c in range(N):
            wait_chunk(c)

    dec_copy.wait()
    for d in range(8):
        both = jnp.concatenate([grad[2 * d], grad[2 * d + 1]], axis=0)
        term = nt_dot(both, dec[:, d * WIDE : (d + 1) * WIDE])
        if d == 0:
            acc[...] = term
        else:
            acc[...] += term
    local_id = ids_ref[...] - j * FEATS
    lane = local_id & 127
    block = local_id >> 7
    chosen = []
    for k in range(2):
        picked = jnp.zeros((TOK, ACT), F32)
        for b in range(8):
            table = acc[k * TOK : (k + 1) * TOK, b * 128 : (b + 1) * 128]
            got = jnp.take_along_axis(table, lane, axis=1)
            picked = jnp.where(block == b, got, picked)
        chosen.append((picked * vals_ref[...]).astype(BF16))
    terms = jnp.concatenate(chosen, axis=0)
    row = lax.broadcasted_iota(jnp.int32, (256, 192), 0)
    col = lax.broadcasted_iota(jnp.int32, (256, 192), 1)
    slot = row & 7
    source = ((row >> 3) & 1) * TOK + (row >> 4) * 6 + slot
    spread = jnp.where((col == source) & (slot < 6), 1.0, 0.0).astype(BF16)
    spread_terms = jnp.dot(spread, terms, preferred_element_type=F32).astype(BF16)
    for q in range(N):
        ed_send[q] = spread_terms[16 * q : 16 * q + 16, :]

    def ed_copy(o):
        p = peer(o)
        return remote(ed_send.at[p], ed_recv.at[j], ed_ssem.at[o], ed_rsem.at[j], s, p)

    @pl.loop(1, N)
    def _(o):
        ed_copy(o).start()

    ed_recv[j] = ed_send[j]

    @pl.loop(1, N)
    def _(o):
        p = peer(o)
        arrived(ed_recv.at[p], ed_rsem.at[p], ed_ssem.at[o])

    edges = jnp.zeros((16, ACT), F32)
    for q in range(N):
        edges += ed_recv[q].astype(F32)
    out_ref[...] = edges

    @pl.loop(1, N)
    def _(o):
        ed_copy(o).wait_send()

    @pl.when(s < TOP)
    def _():
        remote(enc_ref, e1_recv.at[s], e1_ssem, e1_rsem.at[s], TOP, j).wait_send()

        @pl.loop(1, N)
        def _(o):
            chunk_copy(o).wait_send()

    @pl.when(s >= 1)
    def _():
        @pl.loop(1, N)
        def _(o):
            sc_copy(o).wait_send()
            wv_peer_copy(o).wait_send()

        for k in range(2):
            for d in range(8):
                @pl.when(2 * d + k != j)
                def _():
                    v_copy(k, d).wait_send()

        hop_copy().wait_send()


def body(
    attn_logits, out_weight, value_weight, norm_gain, norm_scale, target_encoder,
    target_ids, target_token, decoder, source_ids, source_values,
):
    j = lax.axis_index("tensor")
    picked = jnp.concatenate(
        [lax.dynamic_slice_in_dim(target_encoder, target_ids[k], 1, axis=0) for k in range(2)],
        axis=0,
    ).astype(F32)
    start = 40 * j - 128 * jnp.minimum(40 * j // 128, 3)
    enc = lax.dynamic_update_slice(jnp.zeros((8, 256), F32), picked, (0, start))
    scale = jnp.broadcast_to(jnp.pad(norm_scale[0], (0, 2))[:, None], (8, 128))

    vmem = pl.BlockSpec(memory_space=pltpu.VMEM)
    smem = pl.BlockSpec(memory_space=pltpu.SMEM)
    hbm = pl.BlockSpec(memory_space=pl.ANY)
    dma = pltpu.SemaphoreType.DMA
    out = pl.pallas_call(
        chain_kernel,
        out_shape=jax.ShapeDtypeStruct((16, ACT), F32),
        in_specs=[vmem, vmem, vmem, vmem, smem, vmem, vmem, hbm, hbm, hbm],
        out_specs=vmem,
        scratch_shapes=[
            pltpu.VMEM((512, 5120), BF16),
            pltpu.VMEM((FEATS, 5120), BF16),
            pltpu.VMEM((1024, WIDE), BF16),
            pltpu.VMEM((N, TOK, WIDE), BF16),
            pltpu.VMEM((TOK, WIDE), BF16),
            pltpu.VMEM((2, TOK, HD), BF16),
            pltpu.VMEM((N, TOK, HD), BF16),
            pltpu.VMEM((N, 8, 128), F32),
            pltpu.VMEM((TOK, 128), F32),
            pltpu.VMEM((8, 8, 256), F32),
            pltpu.VMEM((16, 256), BF16),
            pltpu.VMEM((N, 16, 256), BF16),
            pltpu.VMEM((TOK, HEADS_HERE * HD), BF16),
            pltpu.VMEM((HEADS_HERE * HD, HD), BF16),
            pltpu.VMEM((128, 128), F32),
            pltpu.VMEM((2 * TOK, FEATS), F32),
            pltpu.VMEM((N, 16, ACT), BF16),
            pltpu.VMEM((N, 16, ACT), BF16),
            dma((3,)),
            dma((N,)), dma((N,)),
            dma((N,)), dma((N,)),
            dma, dma((8,)),
            dma((N,)), dma((N,)),
            dma((N,)), dma((N,)),
            dma((N,)), dma((N,)),
            dma,
            dma((N,)), dma((N,)),
        ],
        compiler_params=pltpu.CompilerParams(
            collective_id=0, has_side_effects=True, vmem_limit_bytes=48 * 2**20
        ),
        name="chain",
    )(
        enc, scale, attn_logits[0], norm_gain, target_token, source_ids[0], source_values[0],
        out_weight[0], value_weight[0], decoder[0],
    )
    return out.reshape(2, 8, ACT)[:, :6].transpose(1, 0, 2)[None]


def solution(mesh):
    return jax.shard_map(
        body,
        mesh=mesh,
        in_specs=(
            P("section", "tensor", None, None),
            P("section", "tensor", None),
            P("section", "tensor", None),
            P("section", None),
            P("section", "tensor"),
            P(None, ("section", "tensor")),
            P(),
            P(),
            P("section", "tensor", None),
            P("section", None, None),
            P("section", None, None),
        ),
        out_specs=P("section", "tensor", None, None),
        check_vma=False,
    )
```

time: 1640 us -> 251 us (0.15)
  waiting for transfers between devices: 1100 us -> 0 us
  local copies, waits for them, and re-layouts: 278 us -> 11.5 us
  Pallas kernels: 0 us -> 235 us
  blocking collectives: 124 us -> 0 us
  matrix products: 54.6 us -> 0 us
  other arithmetic: 41.5 us -> 0.01 us
  starting transfers between devices: 20.9 us -> 0 us
    while x24 -> x0, waiting for transfers between devices: 699 us -> none
    all_gather x8 -> x0, waiting for transfers between devices: 380 us -> none  [advance(): gathered = lax.all_gather(gradient, 'tensor', axis=0, tiled=True)]
    gather x2 -> x0, local copies, waits for them, and re-layouts: 238 us -> none  [the longest x1 235 us: body(): chosen = jnp.take_along_axis(scores, index_table, axis=2)]
    pallas_call x0 -> x1, Pallas kernels: none -> 235 us  [body(): pl.pallas_call(chain_kernel, out_shape=jax.ShapeDtypeStruct((16, ACT), F3...]
    unnamed x1 -> x0, blocking collectives: 72.5 us -> none
    dot_general x25 -> x0, matrix products: 54.6 us -> none  [the longest x8 39.7 us: pull_back(): jnp.einsum('tkd,ed->tke', gathered, out_rows, preferred_element_type=jnp....]
    all_gather x1 -> x0, blocking collectives: 51.3 us -> none  [body(): lax.all_gather(picked_rows, ('section', 'tensor'), axis=1, tiled=True)]
    convert_element_type x8 -> x0, local copies, waits for them, and re-layouts: 26.6 us -> none  [pull_back(): mixed = lax.psum_scatter(jnp.einsum('tkw,wd->tkd', value_grad, value_rows...]
  transfers between devices with their start and end apart: 32 -> 0, of which waited for: 24 -> 0; matrix products, arithmetic and copies ran while one was open for 1% -> 0% of each run, Pallas kernels for 0% -> 0%
where the time goes in v1:
time: 251 us; the launch traced here: 250 us
  Pallas kernels  235 us (94%)
  local copies, waits for them, and re-layouts  11.5 us (5%)
  between operations  4.03 us (2%)
    pallas_call x1, Pallas kernels, body(): pl.pallas_call(chain_kernel, out_shape=jax.ShapeDtypeStruct((16, ACT), F3...  235 us
    unnamed x17, local copies, waits for them, and re-layouts  8.22 us

profile of v1, /device:TPU:0, one launch (start us, length us, event | category | flops | bytes accessed | tf_op | source)
XLA Modules:
  0.0 250.1 jit_solution(9430865995718804100)
XLA Ops:
  0.0 1.4 fusion
  5.4 0.8 constant_dynamic-slice_fusion.1
  6.2 0.1 copy.15
  6.3 0.1 copy.16
  6.4 0.4 dynamic_update_slice.3.enc_ref
  6.8 0.7 pad.4
  7.4 0.1 broadcast_in_dim.13.scale_ref
  7.5 0.0 copy-start
  7.5 2.5 copy-done
  10.0 0.0 copy-start.1
  10.0 1.1 copy-done.1
  11.1 0.0 copy-start.2
  11.1 0.9 copy-done.2
  12.0 0.0 copy-start.3
  12.0 0.8 copy-done.3
  12.8 0.0 copy-start.4
  12.8 0.8 copy-done.4
  13.6 0.0 copy-start.5
  13.6 0.7 copy-done.5
  14.3 0.0 copy-start.6
  14.3 0.7 copy-done.6
  14.9 234.5 %chain.1 = f32[16,128]{1,0:T(8,128)S(1)} custom-call(f32[8,256]{1,0:T(8,128)S(1)} %dynamic_update_slice.3.enc_ref, f32[8,128]{1,0:T(8,128)S(1)} %broadcast_in_dim.13.scale_ref, bf16[4,96,96]{2,1,0:T(8,128)(2,1)S(1)} %bitcast.18, f32[1,5120]{1,0:T(1,128)S(1)} %copy-done.5, s32[2]{0:T(128)S(1)} %copy-done.6, s32[96,128]{1,0:T(8,128)S(1)} %bitcast.19, ...), custom_call_target="tpu_custom_call" | custom-call | tf_op jit(solution)/shard_map/chain/pallas_call | solution.py:349
  249.5 0.6 copy.19
  (2 shorter events, 0.0 us)
Async XLA Ops:
  7.5 2.5 copy-start
  10.0 1.1 copy-start.1
  11.1 0.9 copy-start.2
  12.0 0.8 copy-start.3
  12.8 0.8 copy-start.4
  13.6 0.7 copy-start.5
  14.3 0.7 copy-start.6

commit v2 on v1

v2 whole, which is shorter than its diff:
```python
import jax
import jax.numpy as jnp
from jax import lax
from jax.experimental import pallas as pl
from jax.experimental.pallas import tpu as pltpu
from jax.sharding import PartitionSpec as P

MESH = pl.DeviceIdType.MESH
F32 = jnp.float32
BF16 = jnp.bfloat16

TOK = 96
N = 16
TOP = 7
HD = 128
WIDE = 640
HEADS_HERE = 4
ACT = 128
FEATS = 1024


def nt_dot(a, b):
    return lax.dot_general(a, b, (((1,), (1,)), ((), ())), preferred_element_type=F32)


def chain_kernel(
    enc_hbm, scale_hbm, logits_hbm, gain_hbm, want_hbm, tok_hbm, ids_hbm, vals_hbm,
    wo_hbm, wv_hbm, dec_hbm,
    out_ref,
    table, scale_raw, logits_ref, gain_up, want_ref, tok_ref, ids_ref, vals_ref,
    enc_ref, scale_ref,
    wo, dec, wvs, wvf, joint, grad, grad_base, grad_own, v_send, v_recv, v_full, base,
    sc_recv, sc_rows, e1_recv, e2_send, e2_recv, pat, hcat, pad, acc, ed_send, ed_recv,
    local_sem, gain_ssem, gain_rsem, wv_ssem, wv_rsem, fw_ssem, fw_rsem, sc_ssem, sc_rsem,
    e1_ssem, e1_rsem, e2_ssem, e2_rsem, v_ssem, v_rsem, g_ssem, g_rsem, hop_ssem, hop_rsem,
    copy_ssem, copy_rsem, ed_ssem, ed_rsem,
):
    s = lax.axis_index("section")
    j = lax.axis_index("tensor")
    my_k = lax.rem(j, 2)
    my_d = j // 2
    row = j // 4
    col = lax.rem(j, 4)
    mine = my_k * 8 + my_d
    below = s - 1
    spreads = (s == 6) | (s == 5) | (s == 3) | (s == 1)
    joins = (s == 4) | (s == 2) | (s == 0)
    feeds_spread = (s == 7) | (s == 6) | (s == 4) | (s == 2)
    feeds_join = (s == 5) | (s == 3) | (s == 1)

    def peer(o):
        return lax.rem(j + o, N)

    def at_row(o):
        return row * 4 + lax.rem(col + o, 4)

    def at_col(o):
        return lax.rem(row + o, 4) * 4 + col

    def chunk_of(p):
        return lax.rem(p, 2) * 8 + p // 2

    def remote(src, dst, ssem, rsem, section, index):
        return pltpu.make_async_remote_copy(
            src_ref=src, dst_ref=dst, send_sem=ssem, recv_sem=rsem,
            device_id=(section, index), device_id_type=MESH,
        )

    def arrived(dst, rsem, ssem):
        remote(dst, dst, ssem, rsem, s, peer(1)).wait_recv()

    barrier = pltpu.get_barrier_semaphore()

    def greet(section, index):
        pl.semaphore_signal(barrier, inc=1, device_id=(section, index), device_id_type=MESH)

    @pl.when(s < TOP - 1)
    def _():
        greet(TOP, j)

    @pl.when(s == TOP)
    def _():
        for q in range(TOP - 1):
            greet(q, j)

    @pl.loop(1, N)
    def _(o):
        greet(s, peer(o))

    @pl.when(s < TOP)
    def _():
        @pl.loop(0, N)
        def _(p):
            greet(s + 1, p)

    @pl.when(s >= 1)
    def _():
        @pl.loop(0, N)
        def _(p):
            greet(below, p)

    small = [
        pltpu.make_async_copy(src, dst, local_sem.at[2 + i])
        for i, (src, dst) in enumerate([
            (want_hbm, want_ref), (enc_hbm, table), (scale_hbm, scale_raw),
            (logits_hbm, logits_ref), (tok_hbm, tok_ref),
            (ids_hbm, ids_ref), (vals_hbm, vals_ref),
        ])
    ]
    for copy in small:
        copy.start()
    wo_copy = pltpu.make_async_copy(wo_hbm, wo, local_sem.at[0])
    wo_copy.start()
    dec_copy = pltpu.make_async_copy(dec_hbm, dec, local_sem.at[1])
    dec_copy.start()

    small[0].wait()
    small[1].wait()
    first_lane = 40 * j - 128 * jnp.minimum((40 * j) // 128, 3)
    spot = lax.broadcasted_iota(jnp.int32, (40, 256), 1) - lax.broadcasted_iota(jnp.int32, (40, 256), 0)
    lane = lax.broadcasted_iota(jnp.int32, (40, 512), 1)

    def pick(i, found):
        part = table[:, pl.ds(pl.multiple_of(i * 512, 512), 512)].astype(F32)
        return tuple(
            found[k] + jnp.where(lane + i * 512 == want_ref[k], part, 0.0) for k in range(2)
        )

    found = lax.fori_loop(0, 32, pick, (jnp.zeros((40, 512), F32),) * 2)
    enc_ref[...] = jnp.zeros_like(enc_ref)
    for k in range(2):
        column = jnp.sum(found[k], axis=1, keepdims=True)
        enc_ref[k : k + 1, :] = jnp.sum(
            jnp.where(spot == first_lane, column, 0.0), axis=0, keepdims=True
        )
    small[2].wait()
    diagonal = lax.broadcasted_iota(jnp.int32, (8, 6), 0) == lax.broadcasted_iota(jnp.int32, (8, 6), 1)
    scale_ref[...] = jnp.broadcast_to(
        jnp.sum(jnp.where(diagonal, scale_raw[...], 0.0), axis=1, keepdims=True), (8, 128)
    )

    pl.semaphore_wait(
        barrier,
        15
        + jnp.where(s >= 1, N, 0)
        + jnp.where(s < TOP, N, 0)
        + jnp.where(s < TOP - 1, 1, 0)
        + jnp.where(s == TOP, TOP - 1, 0),
    )

    def e1_copy():
        return remote(enc_ref, e1_recv.at[s], e1_ssem, e1_rsem.at[s], TOP, j)

    @pl.when(s < TOP)
    def _():
        e1_copy().start()

    def sc_copy(o):
        return remote(scale_ref, sc_recv.at[j], sc_ssem.at[o], sc_rsem.at[j], s, peer(o))

    def gain_copy():
        return remote(gain_hbm, gain_up, gain_ssem, gain_rsem, below, j)

    def wv_copy(p):
        cols = pl.ds(pl.multiple_of((p // 2) * WIDE, 128), WIDE)
        rows = pl.ds(pl.multiple_of(j * 64, 64), 64)
        return remote(
            wv_hbm.at[:, cols], wvs.at[rows], wv_ssem.at[p], wv_rsem.at[j], below, p
        )

    def half_rows(c, h):
        return wvf.at[pl.ds(pl.multiple_of(c * 64 + 32 * h, 32), 32)]

    def full_copy(h, o):
        return remote(
            wv_hbm.at[pl.ds(32 * h, 32)], half_rows(j, h),
            wv_ssem.at[4 * h + o], fw_rsem.at[2 * j + h], below, at_col(o) if h else at_row(o),
        )

    @pl.when(s >= 1)
    def _():
        gain_copy().start()

        @pl.loop(1, N)
        def _(o):
            sc_copy(o).start()

    @pl.when(feeds_spread)
    def _():
        @pl.loop(0, N)
        def _(p):
            wv_copy(p).start()

    @pl.when(feeds_join)
    def _():
        for o in (0, 1, 3, 2):
            for h in range(2):
                full_copy(h, o).start()

    for copy in small[3:]:
        copy.wait()
    pad[...] = jnp.zeros_like(pad)
    hcat[...] = jnp.zeros_like(hcat)
    query = lax.broadcasted_iota(jnp.int32, (TOK, TOK), 0)
    key = lax.broadcasted_iota(jnp.int32, (TOK, TOK), 1)
    for h in range(HEADS_HERE):
        scores = jnp.where(key <= query, logits_ref[h].astype(F32), -jnp.inf)
        highest = jnp.max(scores, axis=-1, keepdims=True)
        weights = jnp.exp(scores - highest)
        pad[0:TOK, 0:TOK] = weights / jnp.sum(weights, axis=-1, keepdims=True)
        pat[:, h * HD : (h + 1) * HD] = pad[...].T[0:TOK, :].astype(BF16)

    def hop_copy(src):
        return remote(src, grad_base, hop_ssem, hop_rsem, below, j)

    @pl.when(s == TOP)
    def _():
        e1_recv[TOP] = enc_ref[...]
        for q in range(TOP):
            arrived(e1_recv.at[q], e1_rsem.at[q], e1_ssem)
        rows = jnp.concatenate([e1_recv[:, 0, :], e1_recv[:, 1, :]], axis=0)
        e2_send[...] = rows.astype(BF16)
        e2_recv[j] = rows.astype(BF16)

        def e2_copy(o):
            return remote(e2_send, e2_recv.at[j], e2_ssem.at[o], e2_rsem.at[j], s, peer(o))

        @pl.loop(1, N)
        def _(o):
            e2_copy(o).start()

        @pl.loop(1, N)
        def _(o):
            p = peer(o)
            arrived(e2_recv.at[p], e2_rsem.at[p], e2_ssem.at[o])

        blocks = [jnp.zeros((16, 128), F32) for _ in range(5)]
        for q in range(N):
            first = min(40 * q // 128, 3)
            piece = e2_recv[q].astype(F32)
            blocks[first] = blocks[first] + piece[:, 0:128]
            blocks[first + 1] = blocks[first + 1] + piece[:, 128:256]
        top_rows = jnp.concatenate(blocks, axis=1)
        token = lax.broadcasted_iota(jnp.int32, (TOK, WIDE), 0)
        for k in range(2):
            hit = token == tok_ref[k]
            for d in range(8):
                one = jnp.broadcast_to(top_rows[k * 8 + d : k * 8 + d + 1, :], (TOK, WIDE))
                grad[8 * k + d] = jnp.where(hit, one, 0.0).astype(BF16)
        hop_copy(grad.at[mine]).start()

        @pl.loop(1, N)
        def _(o):
            e2_copy(o).wait_send()

    forwards = []
    for o in (0, 1, 3, 2):
        forwards.append([(at_row(o), 0, at_col(q), 4 * o + q) for q in (1, 3, 2)])
        forwards.append([(at_col(o), 1, at_row(q), 16 + 4 * o + q) for q in (1, 3, 2)])

    def forward_copy(c, h, to, sem):
        return remote(half_rows(c, h), half_rows(c, h), fw_ssem.at[sem], fw_rsem.at[2 * c + h], s, to)

    @pl.when(joins)
    def _():
        for items in forwards:
            c, h = items[0][0], items[0][1]
            arrived(half_rows(c, h), fw_rsem.at[2 * c + h], fw_ssem.at[0])
            for item in items:
                forward_copy(*item).start()
        arrived(gain_up, gain_rsem, gain_ssem)

        @pl.loop(0, N)
        def _(c):
            @pl.when(c // 4 != row)
            def _():
                arrived(half_rows(c, 0), fw_rsem.at[2 * c], fw_ssem.at[0])

            @pl.when(lax.rem(c, 4) != col)
            def _():
                arrived(half_rows(c, 1), fw_rsem.at[2 * c + 1], fw_ssem.at[0])

        for items in forwards:
            for item in items:
                forward_copy(*item).wait_send()

        @pl.loop(0, 64)
        def _(i):
            part = pl.ds(pl.multiple_of(i * 16, 16), 16)
            wvf[part, :] = (wvf[part, :].astype(F32) * gain_up[...]).astype(BF16)

    wo_copy.wait()
    dec_copy.wait()

    @pl.when((s == 4) | (s == 2))
    def _():
        @pl.loop(0, 4)
        def _(i):
            part = pl.ds(pl.multiple_of(i * 256, 256), 256)
            total = jnp.zeros((256, HEADS_HERE * HD), F32)
            for d in range(8):
                cols = slice(d * WIDE, (d + 1) * WIDE)
                total += nt_dot(wvf[part, cols], wo[:, cols])
            joint[part, 0 : HEADS_HERE * HD] = total.astype(BF16)

    @pl.when(s == 0)
    def _():
        @pl.loop(0, 8)
        def _(i):
            part = pl.ds(pl.multiple_of(i * 128, 128), 128)
            total = jnp.zeros((128, FEATS), F32)
            for d in range(8):
                cols = slice(d * WIDE, (d + 1) * WIDE)
                total += nt_dot(wvf[part, cols], dec[:, cols])
            joint[part, :] = total.astype(BF16)

    @pl.when(s >= 1)
    def _():
        @pl.loop(1, N)
        def _(o):
            p = peer(o)
            arrived(sc_recv.at[p], sc_rsem.at[p], sc_ssem.at[0])

        sc_recv[j] = scale_ref[...]
        for q in range(N):
            sc_rows[6 * q : 6 * q + 6, :] = sc_recv[q, 0:6, :]

    def value_grad(k):
        @pl.loop(0, N)
        def _(p):
            arrived(v_recv.at[k, p], v_rsem.at[k * N + p], v_ssem.at[0])

        pieces = []
        for q in range(8):
            both = v_recv[k, 2 * q].astype(F32) + v_recv[k, 2 * q + 1].astype(F32)
            pieces.append(both.astype(BF16))
        return jnp.concatenate(pieces, axis=1)

    def v_copy(k, p):
        return remote(
            v_send.at[k], v_recv.at[k, j], v_ssem.at[k * N + p], v_rsem.at[k * N + j], below, p
        )

    def send_values(k, head_grad):
        for h in range(HEADS_HERE):
            hcat[h * HD : h * HD + TOK, :] = head_grad[:, h * HD : (h + 1) * HD]
        part = jnp.dot(pat[...], hcat[...], preferred_element_type=F32)
        v_send[k] = (part * sc_rows[...]).astype(BF16)
        for p in range(N):
            @pl.when(feeds_join | (k == p % 2))
            def _():
                v_copy(k, p).start()

    def half_copy(c, h, to, sem):
        part = grad.at[chunk_of(c), pl.ds(48 * h, 48)]
        return remote(part, part, g_ssem.at[sem], g_rsem.at[2 * c + h], s, to)

    def half_arrived(c, h):
        arrived(grad.at[chunk_of(c), pl.ds(48 * h, 48)], g_rsem.at[2 * c + h], g_ssem.at[0])

    own_sends, row_sends, col_sends = [], [], []
    for o in (1, 3, 2):
        own_sends.append((j, 0, at_row(o), o))
        own_sends.append((j, 1, at_col(o), 4 + o))
    for o in (1, 3, 2):
        own_sends.append((j, 0, at_col(o), 8 + o))
        own_sends.append((j, 1, at_row(o), 12 + o))
    for o in (1, 3, 2):
        row_sends.append([(at_row(o), 0, at_col(q), 16 + 4 * o + q) for q in (1, 3, 2)])
        col_sends.append([(at_col(o), 1, at_row(q), 32 + 4 * o + q) for q in (1, 3, 2)])

    own_cols = pl.ds(pl.multiple_of(my_d * WIDE, 128), WIDE)

    def make_chunk():
        mixed = jnp.dot(value_grad(my_k), wvs[...], preferred_element_type=F32)
        grad[mine] = (grad_base[...].astype(F32) + mixed * gain_up[:, own_cols]).astype(BF16)
        for item in own_sends:
            half_copy(*item).start()

        @pl.when(s == 6)
        def _():
            hop_copy(grad.at[mine]).start()

    def forward(k):
        for items in row_sends:
            c = items[0][0]

            @pl.when(lax.rem(c, 2) == k)
            def _():
                half_arrived(c, 0)
                for item in items:
                    half_copy(*item).start()

        @pl.when(my_k == k)
        def _():
            for items in col_sends:
                half_arrived(items[0][0], 1)
                for item in items:
                    half_copy(*item).start()

    def wait_chunk(k, d):
        c = 2 * d + k

        @pl.when(spreads & (c // 4 != row))
        def _():
            half_arrived(c, 0)

        @pl.when(spreads & (lax.rem(c, 4) != col))
        def _():
            half_arrived(c, 1)

    def whole_copy(k):
        part = grad.at[pl.ds(8 * k, 8)]
        return remote(part, part, copy_ssem.at[k], copy_rsem.at[k], below, j)

    @pl.when(spreads)
    def _():
        arrived(gain_up, gain_rsem, gain_ssem)

        @pl.loop(0, N)
        def _(p):
            rows = pl.ds(pl.multiple_of(p * 64, 64), 64)
            arrived(wvs.at[rows], wv_rsem.at[p], wv_ssem.at[0])

        arrived(grad_base, hop_rsem, hop_ssem)

    @pl.when(spreads)
    def _():
        make_chunk()
        forward(0)

        forward(1)


    @pl.when(spreads | (s == TOP))
    def _():
        @pl.loop(0, 2)
        def _(k):
            total = jnp.zeros((TOK, HEADS_HERE * HD), F32)
            for d in range(8):
                wait_chunk(k, d)
                total += nt_dot(grad[8 * k + d], wo[:, d * WIDE : (d + 1) * WIDE])
            send_values(k, total.astype(BF16))

            @pl.when(feeds_join)
            def _():
                whole_copy(k).start()

    @pl.when((s == 4) | (s == 2))
    def _():
        @pl.loop(0, 2)
        def _(k):
            arrived(grad.at[pl.ds(8 * k, 8)], copy_rsem.at[k], copy_ssem.at[0])
            total = jnp.zeros((TOK, HEADS_HERE * HD), F32)
            for d in range(8):
                total += nt_dot(grad[8 * k + d], wo[:, d * WIDE : (d + 1) * WIDE])
            base[...] = total
            values = value_grad(k)
            v_full[k] = values
            total = base[...] + jnp.dot(
                values, joint[:, 0 : HEADS_HERE * HD], preferred_element_type=F32
            )
            send_values(k, total.astype(BF16))

            @pl.when(my_k == k)
            def _():
                mixed = jnp.dot(values, wvf[:, own_cols], preferred_element_type=F32)
                grad_own[...] = (grad[mine].astype(F32) + mixed).astype(BF16)
                hop_copy(grad_own).start()

        @pl.loop(0, 2)
        def _(k):
            for d in range(8):
                mixed = jnp.dot(
                    v_full[k], wvf[:, d * WIDE : (d + 1) * WIDE], preferred_element_type=F32
                )
                grad[8 * k + d] = (grad[8 * k + d].astype(F32) + mixed).astype(BF16)

    @pl.when(s == 0)
    def _():
        for k in range(2):
            arrived(grad.at[pl.ds(8 * k, 8)], copy_rsem.at[k], copy_ssem.at[0])
            part = slice(k * TOK, (k + 1) * TOK)
            for d in range(8):
                term = nt_dot(grad[8 * k + d], dec[:, d * WIDE : (d + 1) * WIDE])
                if d == 0:
                    acc[part, :] = term
                else:
                    acc[part, :] += term
            acc[part, :] += jnp.dot(value_grad(k), joint[...], preferred_element_type=F32)

    @pl.when(s >= 1)
    def _():
        for d in range(8):
            both = jnp.concatenate([grad[d], grad[8 + d]], axis=0)
            term = nt_dot(both, dec[:, d * WIDE : (d + 1) * WIDE])
            if d == 0:
                acc[...] = term
            else:
                acc[...] += term

    local_id = ids_ref[...] - j * FEATS
    lane = local_id & 127
    block = local_id >> 7
    chosen = []
    for k in range(2):
        picked = jnp.zeros((TOK, ACT), F32)
        for b in range(8):
            near = acc[k * TOK : (k + 1) * TOK, b * 128 : (b + 1) * 128]
            got = jnp.take_along_axis(near, lane, axis=1)
            picked = jnp.where(block == b, got, picked)
        chosen.append((picked * vals_ref[...]).astype(BF16))
    terms = jnp.concatenate(chosen, axis=0)
    e_row = lax.broadcasted_iota(jnp.int32, (256, 192), 0)
    e_col = lax.broadcasted_iota(jnp.int32, (256, 192), 1)
    slot = e_row & 7
    source = ((e_row >> 3) & 1) * TOK + (e_row >> 4) * 6 + slot
    placing = jnp.where((e_col == source) & (slot < 6), 1.0, 0.0).astype(BF16)
    placed = jnp.dot(placing, terms, preferred_element_type=F32).astype(BF16)
    for q in range(N):
        ed_send[q] = placed[16 * q : 16 * q + 16, :]

    def ed_copy(o):
        p = peer(o)
        return remote(ed_send.at[p], ed_recv.at[j], ed_ssem.at[o], ed_rsem.at[j], s, p)

    @pl.loop(1, N)
    def _(o):
        ed_copy(o).start()

    ed_recv[j] = ed_send[j]

    @pl.loop(1, N)
    def _(o):
        p = peer(o)
        arrived(ed_recv.at[p], ed_rsem.at[p], ed_ssem.at[o])

    edges = jnp.zeros((16, ACT), F32)
    for q in range(N):
        edges += ed_recv[q].astype(F32)
    out_ref[...] = edges

    @pl.loop(1, N)
    def _(o):
        ed_copy(o).wait_send()

    @pl.when(s < TOP)
    def _():
        e1_copy().wait_send()

    @pl.when(s >= 1)
    def _():
        gain_copy().wait_send()

        @pl.loop(1, N)
        def _(o):
            sc_copy(o).wait_send()

        for k in range(2):
            for p in range(N):
                @pl.when(feeds_join | (k == p % 2))
                def _():
                    v_copy(k, p).wait_send()

    @pl.when(feeds_spread)
    def _():
        hop_copy(grad_own).wait_send()

        @pl.loop(0, N)
        def _(p):
            wv_copy(p).wait_send()

    @pl.when(feeds_join)
    def _():
        for o in range(4):
            for h in range(2):
                full_copy(h, o).wait_send()
        for k in range(2):
            whole_copy(k).wait_send()

    @pl.when(spreads)
    def _():
        for item in own_sends + sum(row_sends, []) + sum(col_sends, []):
            half_copy(*item).wait_send()


def body(
    attn_logits, out_weight, value_weight, norm_gain, norm_scale, target_encoder,
    target_ids, target_token, decoder, source_ids, source_values,
):
    vmem = pl.BlockSpec(memory_space=pltpu.VMEM)
    hbm = pl.BlockSpec(memory_space=pltpu.HBM)
    dma = pltpu.SemaphoreType.DMA
    out = pl.pallas_call(
        chain_kernel,
        out_shape=jax.ShapeDtypeStruct((16, ACT), F32),
        in_specs=[hbm] * 11,
        out_specs=vmem,
        scratch_shapes=[
            pltpu.VMEM((40, 16384), BF16),
            pltpu.VMEM((1, 6), F32),
            pltpu.VMEM((HEADS_HERE, TOK, TOK), BF16),
            pltpu.VMEM((1, 5120), F32),
            pltpu.SMEM((2,), jnp.int32),
            pltpu.SMEM((2,), jnp.int32),
            pltpu.VMEM((TOK, ACT), jnp.int32),
            pltpu.VMEM((TOK, ACT), F32),
            pltpu.VMEM((8, 256), F32),
            pltpu.VMEM((8, 128), F32),
            pltpu.VMEM((512, 5120), BF16),
            pltpu.VMEM((FEATS, 5120), BF16),
            pltpu.VMEM((1024, WIDE), BF16),
            pltpu.VMEM((1024, 5120), BF16),
            pltpu.VMEM((1024, FEATS), BF16),
            pltpu.VMEM((N, TOK, WIDE), BF16),
            pltpu.VMEM((TOK, WIDE), BF16),
            pltpu.VMEM((TOK, WIDE), BF16),
            pltpu.VMEM((2, TOK, HD), BF16),
            pltpu.VMEM((2, N, TOK, HD), BF16),
            pltpu.VMEM((2, TOK, 1024), BF16),
            pltpu.VMEM((TOK, HEADS_HERE * HD), F32),
            pltpu.VMEM((N, 8, 128), F32),
            pltpu.VMEM((TOK, 128), F32),
            pltpu.VMEM((8, 8, 256), F32),
            pltpu.VMEM((16, 256), BF16),
            pltpu.VMEM((N, 16, 256), BF16),
            pltpu.VMEM((TOK, HEADS_HERE * HD), BF16),
            pltpu.VMEM((HEADS_HERE * HD, HD), BF16),
            pltpu.VMEM((128, 128), F32),
            pltpu.VMEM((2 * TOK, FEATS), F32),
            pltpu.VMEM((N, 16, ACT), BF16),
            pltpu.VMEM((N, 16, ACT), BF16),
            dma((9,)),
            dma, dma,
            dma((N,)), dma((N,)),
            dma((2 * N,)), dma((2 * N,)),
            dma((N,)), dma((N,)),
            dma, dma((8,)),
            dma((N,)), dma((N,)),
            dma((2 * N,)), dma((2 * N,)),
            dma((3 * N,)), dma((2 * N,)),
            dma, dma,
            dma((2,)), dma((2,)),
            dma((N,)), dma((N,)),
        ],
        compiler_params=pltpu.CompilerParams(
            collective_id=0, has_side_effects=True, vmem_limit_bytes=63 * 2**20
        ),
        name="chain",
    )(
        target_encoder.T, norm_scale, attn_logits[0], norm_gain, target_ids, target_token,
        source_ids[0], source_values[0],
        out_weight[0], value_weight[0], decoder[0],
    )
    return out.reshape(2, 8, ACT)[:, :6].transpose(1, 0, 2)[None]


def solution(mesh):
    return jax.shard_map(
        body,
        mesh=mesh,
        in_specs=(
            P("section", "tensor", None, None),
            P("section", "tensor", None),
            P("section", "tensor", None),
            P("section", None),
            P("section", "tensor"),
            P(None, ("section", "tensor")),
            P(),
            P(),
            P("section", "tensor", None),
            P("section", None, None),
            P("section", None, None),
        ),
        out_specs=P("section", "tensor", None, None),
        check_vma=False,
    )
```

time: 251 us -> 147 us (0.59)
  Pallas kernels: 235 us -> 146 us
  local copies, waits for them, and re-layouts: 11.5 us -> 1.29 us
  between operations: 4.03 us -> 0.01 us
    pallas_call x1, Pallas kernels: 235 us -> 146 us  [body(): pl.pallas_call(chain_kernel, out_shape=jax.ShapeDtypeStruct((16, ACT), F3...]
    unnamed x17 -> x1, local copies, waits for them, and re-layouts: 8.22 us -> 1.29 us
where the time goes in v2:
time: 147 us
  Pallas kernels  146 us (99%)
    pallas_call x1, Pallas kernels, body(): pl.pallas_call(chain_kernel, out_shape=jax.ShapeDtypeStruct((16, ACT), F3...  146 us

profile of v2, /device:TPU:0, one launch (start us, length us, event | category | flops | bytes accessed | tf_op | source)
XLA Modules:
  0.0 147.3 jit_solution(17021367247872530398)
XLA Ops:
  0.0 146.0 %chain.1 = f32[16,128]{1,0:T(8,128)} custom-call(bf16[40,16384]{1,0:T(8,128)(2,1)} %bitcast.16, f32[1,6]{1,0:T(1,128)} %scale_hbm.1, bf16[4,96,96]{2,1,0:T(8,128)(2,1)} %bitcast.18, f32[1,5120]{1,0:T(1,128)} %gain_hbm.1, s32[2]{0:T(128)} %want_hbm.1, s32[2]{0:T(128)} %tok_hbm.1, s32[96,128]{1,0:T(8,128)} %bitcast.19, f32[96,128]{1,0:T(8,128)} %bitcast.20, ...), custom_call_target="tpu_custom_call" | custom-call | tf_op jit(solution)/shard_map/chain/pallas_call | solution.py:594
  146.0 1.3 copy.15

commit v3 on v2

--- a/solution.py
+++ b/solution.py
@@ -17,6 +17,10 @@
 HEADS_HERE = 4
 ACT = 128
 FEATS = 1024
+FAR_FIRST = sorted(
+    [(dy, dx) for dy in range(4) for dx in range(4)],
+    key=lambda at: -min(at[0], 4 - at[0]) - min(at[1], 4 - at[1]),
+)
 
 
 def nt_dot(a, b):
@@ -29,11 +33,13 @@
     out_ref,
     table, scale_raw, logits_ref, gain_up, want_ref, tok_ref, ids_ref, vals_ref,
     enc_ref, scale_ref,
-    wo, dec, wvs, wvf, joint, grad, grad_base, grad_own, v_send, v_recv, v_full, base,
+    wo, wo_t, dec, wvs, wvf, joint, grad, grad_base, grad_own, v_send, v_recv, v_full, base,
     sc_recv, sc_rows, e1_recv, e2_send, e2_recv, pat, hcat, pad, acc, ed_send, ed_recv,
     local_sem, gain_ssem, gain_rsem, wv_ssem, wv_rsem, fw_ssem, fw_rsem, sc_ssem, sc_rsem,
     e1_ssem, e1_rsem, e2_ssem, e2_rsem, v_ssem, v_rsem, g_ssem, g_rsem, hop_ssem, hop_rsem,
     copy_ssem, copy_rsem, ed_ssem, ed_rsem,
+    seeds, u_rows, u_send, u_recv, mix_send, mix_recv, mix,
+    wv_stage, stage_ssem, stage_rsem, pair_ssem, pair_rsem, u_ssem, u_rsem, mix_ssem, mix_rsem, seed_ssem, seed_rsem,
 ):
     s = lax.axis_index("section")
     j = lax.axis_index("tensor")
@@ -41,24 +47,29 @@
     my_d = j // 2
     row = j // 4
     col = lax.rem(j, 4)
-    mine = my_k * 8 + my_d
     below = s - 1
-    spreads = (s == 6) | (s == 5) | (s == 3) | (s == 1)
-    joins = (s == 4) | (s == 2) | (s == 0)
-    feeds_spread = (s == 7) | (s == 6) | (s == 4) | (s == 2)
-    feeds_join = (s == 5) | (s == 3) | (s == 1)
+    spreads = (s == 5) | (s == 4) | (s == 3) | (s == 1)
+    joins = (s == 2) | (s == 0)
+    second = s == TOP - 1
+    feeds_spread = (s == 6) | (s == 5) | (s == 4) | (s == 2)
+    feeds_join = (s == 3) | (s == 1)
 
     def peer(o):
         return lax.rem(j + o, N)
 
+    def far_first(body):
+        for dy, dx in FAR_FIRST:
+            body(lax.rem(row + dy, 4) * 4 + lax.rem(col + dx, 4))
+
+    def far_first_peers(body):
+        for dy, dx in FAR_FIRST[:-1]:
+            body(lax.rem(row + dy, 4) * 4 + lax.rem(col + dx, 4))
+
     def at_row(o):
         return row * 4 + lax.rem(col + o, 4)
 
     def at_col(o):
         return lax.rem(row + o, 4) * 4 + col
-
-    def chunk_of(p):
-        return lax.rem(p, 2) * 8 + p // 2
 
     def remote(src, dst, ssem, rsem, section, index):
         return pltpu.make_async_remote_copy(
@@ -161,12 +172,19 @@
     def gain_copy():
         return remote(gain_hbm, gain_up, gain_ssem, gain_rsem, below, j)
 
-    def wv_copy(p):
-        cols = pl.ds(pl.multiple_of((p // 2) * WIDE, 128), WIDE)
-        rows = pl.ds(pl.multiple_of(j * 64, 64), 64)
-        return remote(
-            wv_hbm.at[:, cols], wvs.at[rows], wv_ssem.at[p], wv_rsem.at[j], below, p
-        )
+    def stage_copy():
+        return remote(wv_hbm, wv_stage, stage_ssem, stage_rsem, below, j)
+
+    own_rows = pl.ds(pl.multiple_of(j * 64, 64), 64)
+
+    def columns_of(p):
+        return wv_stage.at[:, pl.ds(pl.multiple_of((p // 2) * WIDE, 128), WIDE)]
+
+    def wv_copy(o):
+        p = peer(o)
+        return remote(columns_of(p), wvs.at[own_rows], wv_ssem.at[o], wv_rsem.at[j], s, p)
+
+    own_columns = pltpu.make_async_copy(columns_of(j), wvs.at[own_rows], local_sem.at[11])
 
     def half_rows(c, h):
         return wvf.at[pl.ds(pl.multiple_of(c * 64 + 32 * h, 32), 32)]
@@ -177,23 +195,46 @@
             wv_ssem.at[4 * h + o], fw_rsem.at[2 * j + h], below, at_col(o) if h else at_row(o),
         )
 
+    def pair_rows(h, k):
+        return wvf.at[pl.ds(pl.multiple_of(k * 64 + 32 * h, 32), 32)]
+
+    def pair_copy(h):
+        return remote(
+            wv_hbm.at[pl.ds(32 * h, 32)], pair_rows(h, my_k),
+            pair_ssem.at[h], pair_rsem.at[h], s, j + 1 - 2 * my_k,
+        )
+
+    own_wv = pltpu.make_async_copy(
+        wv_hbm, wvf.at[pl.ds(pl.multiple_of(my_k * 64, 64), 64)], local_sem.at[9]
+    )
+    own_gain = pltpu.make_async_copy(gain_hbm, gain_up, local_sem.at[10])
+
+    @pl.when(s == TOP)
+    def _():
+        own_wv.start()
+        own_gain.start()
+
+    @pl.when((s >= 1) & (s < TOP))
+    def _():
+        gain_copy().start()
+
     @pl.when(s >= 1)
     def _():
-        gain_copy().start()
-
         @pl.loop(1, N)
         def _(o):
             sc_copy(o).start()
 
+    @pl.when(s == TOP)
+    def _():
+        pair_copy(0).start()
+
     @pl.when(feeds_spread)
     def _():
-        @pl.loop(0, N)
-        def _(p):
-            wv_copy(p).start()
+        stage_copy().start()
 
     @pl.when(feeds_join)
     def _():
-        for o in (0, 1, 3, 2):
+        for o in (2, 1, 3, 0):
             for h in range(2):
                 full_copy(h, o).start()
 
@@ -210,6 +251,38 @@
         pad[0:TOK, 0:TOK] = weights / jnp.sum(weights, axis=-1, keepdims=True)
         pat[:, h * HD : (h + 1) * HD] = pad[...].T[0:TOK, :].astype(BF16)
 
+    @pl.when(spreads)
+    def _():
+        arrived(wv_stage, stage_rsem, stage_ssem)
+        own_columns.start()
+
+        @pl.loop(1, N)
+        def _(o):
+            wv_copy(o).start()
+
+    def u_copy(h, o):
+        part = u_recv.at[j, :, pl.ds(1280 * h, 1280)]
+        return remote(
+            u_send.at[:, pl.ds(1280 * h, 1280)], part,
+            u_ssem.at[4 * h + o], u_rsem.at[2 * j + h], below, at_col(o) if h else at_row(o),
+        )
+
+    def mix_copy(p):
+        return remote(mix_send, mix_recv.at[j], mix_ssem.at[p], mix_rsem.at[j], below, p)
+
+    def spread_scales():
+        @pl.loop(1, N)
+        def _(o):
+            p = peer(o)
+            arrived(sc_recv.at[p], sc_rsem.at[p], sc_ssem.at[0])
+
+        sc_recv[j] = scale_ref[...]
+        for q in range(N):
+            sc_rows[6 * q : 6 * q + 6, :] = sc_recv[q, 0:6, :]
+
+    def seed_copy():
+        return remote(seeds, u_recv.at[N], seed_ssem, seed_rsem, below, j)
+
     def hop_copy(src):
         return remote(src, grad_base, hop_ssem, hop_rsem, below, j)
 
@@ -223,11 +296,22 @@
         e2_recv[j] = rows.astype(BF16)
 
         def e2_copy(o):
-            return remote(e2_send, e2_recv.at[j], e2_ssem.at[o], e2_rsem.at[j], s, peer(o))
-
-        @pl.loop(1, N)
-        def _(o):
-            e2_copy(o).start()
+            return remote(e2_send, e2_recv.at[j], e2_ssem.at[o], e2_rsem.at[j], s, o)
+
+        far_first_peers(lambda p: e2_copy(p).start())
+
+        pair_copy(1).start()
+        spread_scales()
+        lane = lax.broadcasted_iota(jnp.int32, (TOK, HEADS_HERE * HD), 1)
+        place = lax.broadcasted_iota(jnp.int32, (TOK, HD), 1) - 16 * lax.rem(j, 8)
+        slab = jnp.zeros((TOK, HD), F32)
+        for k in range(2):
+            for h in range(HEADS_HERE):
+                hit = lane == h * HD + tok_ref[k]
+                chosen = jnp.sum(jnp.where(hit, pat[...].astype(F32), 0.0), axis=1, keepdims=True)
+                spot = 4 * k + h
+                slab = slab + jnp.where((place == spot) | (place == spot + 8), chosen, 0.0)
+        mix_send[...] = (slab * sc_rows[...]).astype(BF16)
 
         @pl.loop(1, N)
         def _(o):
@@ -241,22 +325,60 @@
             blocks[first] = blocks[first] + piece[:, 0:128]
             blocks[first + 1] = blocks[first + 1] + piece[:, 128:256]
         top_rows = jnp.concatenate(blocks, axis=1)
+        seeds[...] = jnp.zeros_like(seeds)
+        for d in range(4):
+            cols = slice(d * WIDE, (d + 1) * WIDE)
+            for k in range(2):
+                low = top_rows[k * 8 + d : k * 8 + d + 1, :]
+                high = top_rows[k * 8 + d + 4 : k * 8 + d + 5, :]
+                seeds[k : k + 1, cols] = low.astype(BF16)
+                seeds[8 + k : 9 + k, cols] = high.astype(BF16)
+        seed_copy().start()
+        wo_copy.wait()
+        half = 2560
+        low = nt_dot(seeds[...], wo[:, 0:half])
+        high = nt_dot(seeds[...], wo[:, half:])
+        rows = low[0:2] + high[8:10]
+        parts = [
+            rows[k : k + 1, h * HD : (h + 1) * HD] for k in range(2) for h in range(HEADS_HERE)
+        ]
+        head_rows = jnp.concatenate(parts, axis=0).astype(BF16)
+        own_wv.wait()
+        own_gain.wait()
+        for h in range(2):
+            arrived(pair_rows(h, 1 - my_k), pair_rsem.at[h], pair_ssem.at[h])
+        for h in range(2):
+            cols = slice(h * half, (h + 1) * half)
+            mixed = jnp.dot(head_rows, wvf[0:128, cols], preferred_element_type=F32)
+            u_rows[8 * h : 8 * h + 8, :] = mixed * gain_up[:, cols]
+        u_send[...] = u_rows[...].astype(BF16)
+        for o in (2, 1, 3, 0):
+            for h in range(2):
+                u_copy(h, o).start()
+
+        @pl.loop(0, N)
+        def _(p):
+            mix_copy(p).start()
+
         token = lax.broadcasted_iota(jnp.int32, (TOK, WIDE), 0)
         for k in range(2):
             hit = token == tok_ref[k]
             for d in range(8):
                 one = jnp.broadcast_to(top_rows[k * 8 + d : k * 8 + d + 1, :], (TOK, WIDE))
-                grad[8 * k + d] = jnp.where(hit, one, 0.0).astype(BF16)
-        hop_copy(grad.at[mine]).start()
+                grad[2 * d + k] = jnp.where(hit, one, 0.0).astype(BF16)
 
         @pl.loop(1, N)
         def _(o):
-            e2_copy(o).wait_send()
+            e2_copy(peer(o)).wait_send()
+
+    @pl.when((s >= 1) & (s < TOP))
+    def _():
+        spread_scales()
 
     forwards = []
     for o in (0, 1, 3, 2):
-        forwards.append([(at_row(o), 0, at_col(q), 4 * o + q) for q in (1, 3, 2)])
-        forwards.append([(at_col(o), 1, at_row(q), 16 + 4 * o + q) for q in (1, 3, 2)])
+        forwards.append([(at_row(o), 0, at_col(q), 4 * o + q) for q in (2, 1, 3)])
+        forwards.append([(at_col(o), 1, at_row(q), 16 + 4 * o + q) for q in (2, 1, 3)])
 
     def forward_copy(c, h, to, sem):
         return remote(half_rows(c, h), half_rows(c, h), fw_ssem.at[sem], fw_rsem.at[2 * c + h], s, to)
@@ -289,10 +411,20 @@
             part = pl.ds(pl.multiple_of(i * 16, 16), 16)
             wvf[part, :] = (wvf[part, :].astype(F32) * gain_up[...]).astype(BF16)
 
-    wo_copy.wait()
+    @pl.when(s < TOP)
+    def _():
+        wo_copy.wait()
+
     dec_copy.wait()
 
-    @pl.when((s == 4) | (s == 2))
+    @pl.when(spreads)
+    def _():
+        @pl.loop(0, 40)
+        def _(i):
+            part = pl.ds(pl.multiple_of(i * 128, 128), 128)
+            wo_t[part, :] = wo[:, part].T
+
+    @pl.when(s == 2)
     def _():
         @pl.loop(0, 4)
         def _(i):
@@ -314,72 +446,78 @@
                 total += nt_dot(wvf[part, cols], dec[:, cols])
             joint[part, :] = total.astype(BF16)
 
-    @pl.when(s >= 1)
-    def _():
-        @pl.loop(1, N)
-        def _(o):
-            p = peer(o)
-            arrived(sc_recv.at[p], sc_rsem.at[p], sc_ssem.at[0])
-
-        sc_recv[j] = scale_ref[...]
-        for q in range(N):
-            sc_rows[6 * q : 6 * q + 6, :] = sc_recv[q, 0:6, :]
-
-    def value_grad(k):
+    def wait_values():
         @pl.loop(0, N)
         def _(p):
-            arrived(v_recv.at[k, p], v_rsem.at[k * N + p], v_ssem.at[0])
-
+            @pl.when(spreads)
+            def _():
+                arrived(v_recv.at[p, 0], v_rsem.at[p], v_ssem.at[0])
+
+            @pl.when(joins)
+            def _():
+                arrived(v_recv.at[p], v_rsem.at[p], v_ssem.at[0])
+
+    def value_grad(k):
         pieces = []
         for q in range(8):
-            both = v_recv[k, 2 * q].astype(F32) + v_recv[k, 2 * q + 1].astype(F32)
+            both = v_recv[2 * q, k].astype(F32) + v_recv[2 * q + 1, k].astype(F32)
             pieces.append(both.astype(BF16))
         return jnp.concatenate(pieces, axis=1)
 
-    def v_copy(k, p):
-        return remote(
-            v_send.at[k], v_recv.at[k, j], v_ssem.at[k * N + p], v_rsem.at[k * N + j], below, p
-        )
-
-    def send_values(k, head_grad):
-        for h in range(HEADS_HERE):
-            hcat[h * HD : h * HD + TOK, :] = head_grad[:, h * HD : (h + 1) * HD]
+    def v_copy_both(p):
+        return remote(v_send, v_recv.at[j], v_ssem.at[p], v_rsem.at[j], below, p)
+
+    def v_copy_one(p):
+        return remote(v_send.at[lax.rem(p, 2)], v_recv.at[j, 0], v_ssem.at[p], v_rsem.at[j], below, p)
+
+    def send_values(head_grad):
+        for k in range(2):
+            for h in range(HEADS_HERE):
+                hcat[h * HD : h * HD + TOK, k * HD : (k + 1) * HD] = head_grad[
+                    k * TOK : (k + 1) * TOK, h * HD : (h + 1) * HD
+                ]
         part = jnp.dot(pat[...], hcat[...], preferred_element_type=F32)
-        v_send[k] = (part * sc_rows[...]).astype(BF16)
-        for p in range(N):
-            @pl.when(feeds_join | (k == p % 2))
-            def _():
-                v_copy(k, p).start()
+        for k in range(2):
+            v_send[k] = (part[:, k * HD : (k + 1) * HD] * sc_rows[...]).astype(BF16)
+
+        @pl.when(feeds_join)
+        def _():
+            far_first(lambda p: v_copy_both(p).start())
+
+        @pl.when(feeds_spread)
+        def _():
+            far_first(lambda p: v_copy_one(p).start())
 
     def half_copy(c, h, to, sem):
-        part = grad.at[chunk_of(c), pl.ds(48 * h, 48)]
+        part = grad.at[c, pl.ds(48 * h, 48)]
         return remote(part, part, g_ssem.at[sem], g_rsem.at[2 * c + h], s, to)
 
     def half_arrived(c, h):
-        arrived(grad.at[chunk_of(c), pl.ds(48 * h, 48)], g_rsem.at[2 * c + h], g_ssem.at[0])
+        arrived(grad.at[c, pl.ds(48 * h, 48)], g_rsem.at[2 * c + h], g_ssem.at[0])
 
     own_sends, row_sends, col_sends = [], [], []
-    for o in (1, 3, 2):
+    for o in (2, 1, 3):
         own_sends.append((j, 0, at_row(o), o))
         own_sends.append((j, 1, at_col(o), 4 + o))
-    for o in (1, 3, 2):
+    for o in (2, 1, 3):
         own_sends.append((j, 0, at_col(o), 8 + o))
         own_sends.append((j, 1, at_row(o), 12 + o))
     for o in (1, 3, 2):
-        row_sends.append([(at_row(o), 0, at_col(q), 16 + 4 * o + q) for q in (1, 3, 2)])
-        col_sends.append([(at_col(o), 1, at_row(q), 32 + 4 * o + q) for q in (1, 3, 2)])
+        row_sends.append([(at_row(o), 0, at_col(q), 16 + 4 * o + q) for q in (2, 1, 3)])
+        col_sends.append([(at_col(o), 1, at_row(q), 32 + 4 * o + q) for q in (2, 1, 3)])
 
     own_cols = pl.ds(pl.multiple_of(my_d * WIDE, 128), WIDE)
 
     def make_chunk():
-        mixed = jnp.dot(value_grad(my_k), wvs[...], preferred_element_type=F32)
-        grad[mine] = (grad_base[...].astype(F32) + mixed * gain_up[:, own_cols]).astype(BF16)
+        wait_values()
+        mixed = jnp.dot(value_grad(0), wvs[...], preferred_element_type=F32)
+        grad[j] = (grad_base[...].astype(F32) + mixed * gain_up[:, own_cols]).astype(BF16)
         for item in own_sends:
             half_copy(*item).start()
 
-        @pl.when(s == 6)
+        @pl.when(feeds_spread)
         def _():
-            hop_copy(grad.at[mine]).start()
+            hop_copy(grad.at[j]).start()
 
     def forward(k):
         for items in row_sends:
@@ -398,106 +536,178 @@
                 for item in items:
                     half_copy(*item).start()
 
-    def wait_chunk(k, d):
-        c = 2 * d + k
-
-        @pl.when(spreads & (c // 4 != row))
+    def wait_chunk(c):
+        @pl.when(c // 4 != row)
         def _():
             half_arrived(c, 0)
 
-        @pl.when(spreads & (lax.rem(c, 4) != col))
+        @pl.when(c % 4 != col)
         def _():
             half_arrived(c, 1)
 
-    def whole_copy(k):
-        part = grad.at[pl.ds(8 * k, 8)]
-        return remote(part, part, copy_ssem.at[k], copy_rsem.at[k], below, j)
+    def whole_copy(d):
+        part = grad.at[pl.ds(2 * d, 2)]
+        return remote(part, part, copy_ssem.at[d], copy_rsem.at[d], below, j)
+
+    def whole_arrived(d):
+        arrived(grad.at[pl.ds(2 * d, 2)], copy_rsem.at[d], copy_ssem.at[0])
+
+    def head_grad_of(at_chunk, dot):
+        total = jnp.zeros((2 * TOK, HEADS_HERE * HD), F32)
+        for d in range(8):
+            at_chunk(d)
+            both = grad[2 * d : 2 * d + 2].reshape(2 * TOK, WIDE)
+            total += dot(both, slice(d * WIDE, (d + 1) * WIDE))
+        return total
 
     @pl.when(spreads)
     def _():
         arrived(gain_up, gain_rsem, gain_ssem)
+        own_columns.wait()
+
+        @pl.loop(1, N)
+        def _(o):
+            p = peer(o)
+            rows = pl.ds(pl.multiple_of(p * 64, 64), 64)
+            arrived(wvs.at[rows], wv_rsem.at[p], wv_ssem.at[0])
+
+        arrived(grad_base, hop_rsem, hop_ssem)
+
+    @pl.when(spreads)
+    def _():
+        make_chunk()
+        forward(0)
+        forward(1)
+
+        def take_chunks(d):
+            wait_chunk(2 * d)
+            wait_chunk(2 * d + 1)
+
+            @pl.when(feeds_join)
+            def _():
+                whole_copy(d).start()
+
+        send_values(head_grad_of(
+            take_chunks,
+            lambda both, part: jnp.dot(both, wo_t[part, :], preferred_element_type=F32),
+        ).astype(BF16))
+
+    u_forwards = []
+    for o in (0, 1, 3, 2):
+        u_forwards.append([(at_row(o), 0, at_col(q), 8 + 4 * o + q) for q in (2, 1, 3)])
+        u_forwards.append([(at_col(o), 1, at_row(q), 24 + 4 * o + q) for q in (2, 1, 3)])
+
+    def u_half(c, h):
+        return u_recv.at[c, :, pl.ds(1280 * h, 1280)]
+
+    def u_forward(c, h, to, sem):
+        return remote(u_half(c, h), u_half(c, h), u_ssem.at[sem], u_rsem.at[2 * c + h], s, to)
+
+    @pl.when(second)
+    def _():
+        for items in u_forwards:
+            c, h = items[0][0], items[0][1]
+            arrived(u_half(c, h), u_rsem.at[2 * c + h], u_ssem.at[0])
+            for item in items:
+                u_forward(*item).start()
 
         @pl.loop(0, N)
         def _(p):
-            rows = pl.ds(pl.multiple_of(p * 64, 64), 64)
-            arrived(wvs.at[rows], wv_rsem.at[p], wv_ssem.at[0])
-
-        arrived(grad_base, hop_rsem, hop_ssem)
-
-    @pl.when(spreads)
-    def _():
-        make_chunk()
-        forward(0)
-
-        forward(1)
-
-
-    @pl.when(spreads | (s == TOP))
-    def _():
-        @pl.loop(0, 2)
-        def _(k):
-            total = jnp.zeros((TOK, HEADS_HERE * HD), F32)
-            for d in range(8):
-                wait_chunk(k, d)
-                total += nt_dot(grad[8 * k + d], wo[:, d * WIDE : (d + 1) * WIDE])
-            send_values(k, total.astype(BF16))
-
-            @pl.when(feeds_join)
+            arrived(mix_recv.at[p], mix_rsem.at[p], mix_ssem.at[0])
+
+        arrived(u_recv.at[N], seed_rsem, seed_ssem)
+        kind = lax.broadcasted_iota(jnp.int32, (TOK, HD), 1) & 15
+        for t in range(2):
+            tile = jnp.zeros((TOK, HD), F32)
+            for q in range(8):
+                tile = tile + mix_recv[8 * t + q].astype(F32)
+            for h in range(2):
+                for k in range(2):
+                    keep = (kind >> 2) == 2 * h + k
+                    mix[h, k * TOK : (k + 1) * TOK, t * HD : (t + 1) * HD] = jnp.where(
+                        keep, tile, 0.0
+                    ).astype(BF16)
+
+        @pl.loop(0, N)
+        def _(c):
+            @pl.when(c // 4 != row)
             def _():
-                whole_copy(k).start()
-
-    @pl.when((s == 4) | (s == 2))
-    def _():
-        @pl.loop(0, 2)
-        def _(k):
-            arrived(grad.at[pl.ds(8 * k, 8)], copy_rsem.at[k], copy_ssem.at[0])
-            total = jnp.zeros((TOK, HEADS_HERE * HD), F32)
-            for d in range(8):
-                total += nt_dot(grad[8 * k + d], wo[:, d * WIDE : (d + 1) * WIDE])
-            base[...] = total
-            values = value_grad(k)
-            v_full[k] = values
-            total = base[...] + jnp.dot(
-                values, joint[:, 0 : HEADS_HERE * HD], preferred_element_type=F32
+                arrived(u_half(c, 0), u_rsem.at[2 * c], u_ssem.at[0])
+
+            @pl.when(lax.rem(c, 4) != col)
+            def _():
+                arrived(u_half(c, 1), u_rsem.at[2 * c + 1], u_ssem.at[0])
+
+        half = 2560
+        flat = u_recv[...].reshape(16 * (N + 1), half)
+        low = nt_dot(flat, wo[:, 0:half])
+        high = nt_dot(flat, wo[:, half:])
+        total = jnp.dot(mix[0], low[0:256].astype(BF16), preferred_element_type=F32)
+        total += jnp.dot(mix[1], high[0:256].astype(BF16), preferred_element_type=F32)
+        token = lax.broadcasted_iota(jnp.int32, (TOK, HEADS_HERE * HD), 0)
+        parts = []
+        for k in range(2):
+            one = low[256 + k : 257 + k] + high[264 + k : 265 + k]
+            parts.append(
+                total[k * TOK : (k + 1) * TOK] + jnp.where(token == tok_ref[k], one, 0.0)
             )
-            send_values(k, total.astype(BF16))
-
-            @pl.when(my_k == k)
-            def _():
-                mixed = jnp.dot(values, wvf[:, own_cols], preferred_element_type=F32)
-                grad_own[...] = (grad[mine].astype(F32) + mixed).astype(BF16)
-                hop_copy(grad_own).start()
-
-        @pl.loop(0, 2)
-        def _(k):
-            for d in range(8):
-                mixed = jnp.dot(
-                    v_full[k], wvf[:, d * WIDE : (d + 1) * WIDE], preferred_element_type=F32
-                )
-                grad[8 * k + d] = (grad[8 * k + d].astype(F32) + mixed).astype(BF16)
+        send_values(jnp.concatenate(parts, axis=0).astype(BF16))
+        token = lax.broadcasted_iota(jnp.int32, (TOK, WIDE), 0)
+        for d in range(8):
+            h, cols = d // 4, slice((d % 4) * WIDE, (d % 4 + 1) * WIDE)
+            head_rows = u_recv[0:N, :, cols].reshape(16 * N, WIDE)
+            mixed = jnp.dot(mix[h], head_rows, preferred_element_type=F32)
+            for k in range(2):
+                one = u_recv[N, 8 * h + k : 8 * h + k + 1, cols].astype(F32)
+                grad[2 * d + k] = (
+                    mixed[k * TOK : (k + 1) * TOK] + jnp.where(token == tok_ref[k], one, 0.0)
+                ).astype(BF16)
+        hop_copy(grad.at[j]).start()
+
+    @pl.when(s == 2)
+    def _():
+        base[...] = head_grad_of(whole_arrived, lambda both, part: nt_dot(both, wo[:, part]))
+        wait_values()
+        for k in range(2):
+            v_full[k * TOK : (k + 1) * TOK, :] = value_grad(k)
+        total = base[...] + jnp.dot(
+            v_full[...], joint[:, 0 : HEADS_HERE * HD], preferred_element_type=F32
+        )
+        send_values(total.astype(BF16))
+        mixed = jnp.dot(
+            v_full[pl.ds(pl.multiple_of(my_k * TOK, TOK), TOK), :], wvf[:, own_cols],
+            preferred_element_type=F32,
+        )
+        grad_own[...] = (grad[j].astype(F32) + mixed).astype(BF16)
+        hop_copy(grad_own).start()
+        for d in range(8):
+            mixed = jnp.dot(
+                v_full[...], wvf[:, d * WIDE : (d + 1) * WIDE], preferred_element_type=F32
+            )
+            for k in range(2):
+                grad[2 * d + k] = (
+                    grad[2 * d + k].astype(F32) + mixed[k * TOK : (k + 1) * TOK]
+                ).astype(BF16)
 
     @pl.when(s == 0)
     def _():
+        for d in range(8):
+            whole_arrived(d)
+
+    for d in range(8):
+        both = grad[2 * d : 2 * d + 2].reshape(2 * TOK, WIDE)
+        term = nt_dot(both, dec[:, d * WIDE : (d + 1) * WIDE])
+        if d == 0:
+            acc[...] = term
+        else:
+            acc[...] += term
+
+    @pl.when(s == 0)
+    def _():
+        wait_values()
         for k in range(2):
-            arrived(grad.at[pl.ds(8 * k, 8)], copy_rsem.at[k], copy_ssem.at[0])
-            part = slice(k * TOK, (k + 1) * TOK)
-            for d in range(8):
-                term = nt_dot(grad[8 * k + d], dec[:, d * WIDE : (d + 1) * WIDE])
-                if d == 0:
-                    acc[part, :] = term
-                else:
-                    acc[part, :] += term
-            acc[part, :] += jnp.dot(value_grad(k), joint[...], preferred_element_type=F32)
-
-    @pl.when(s >= 1)
-    def _():
-        for d in range(8):
-            both = jnp.concatenate([grad[d], grad[8 + d]], axis=0)
-            term = nt_dot(both, dec[:, d * WIDE : (d + 1) * WIDE])
-            if d == 0:
-                acc[...] = term
-            else:
-                acc[...] += term
+            v_full[k * TOK : (k + 1) * TOK, :] = value_grad(k)
+        acc[...] += jnp.dot(v_full[...], joint[...], preferred_element_type=F32)
 
     local_id = ids_ref[...] - j * FEATS
     lane = local_id & 127
@@ -520,29 +730,28 @@
     for q in range(N):
         ed_send[q] = placed[16 * q : 16 * q + 16, :]
 
-    def ed_copy(o):
-        p = peer(o)
-        return remote(ed_send.at[p], ed_recv.at[j], ed_ssem.at[o], ed_rsem.at[j], s, p)
-
-    @pl.loop(1, N)
-    def _(o):
-        ed_copy(o).start()
+    def ed_copy(p):
+        return remote(ed_send.at[p], ed_recv.at[j], ed_ssem.at[p], ed_rsem.at[j], s, p)
+
+    far_first_peers(lambda p: ed_copy(p).start())
 
     ed_recv[j] = ed_send[j]
 
     @pl.loop(1, N)
     def _(o):
         p = peer(o)
-        arrived(ed_recv.at[p], ed_rsem.at[p], ed_ssem.at[o])
+        arrived(ed_recv.at[p], ed_rsem.at[p], ed_ssem.at[0])
 
     edges = jnp.zeros((16, ACT), F32)
     for q in range(N):
         edges += ed_recv[q].astype(F32)
-    out_ref[...] = edges
+    for k in range(2):
+        for t in range(6):
+            out_ref[t, k : k + 1, :] = edges[8 * k + t : 8 * k + t + 1, :]
 
     @pl.loop(1, N)
     def _(o):
-        ed_copy(o).wait_send()
+        ed_copy(peer(o)).wait_send()
 
     @pl.when(s < TOP)
     def _():
@@ -550,36 +759,61 @@
 
     @pl.when(s >= 1)
     def _():
-        gain_copy().wait_send()
-
         @pl.loop(1, N)
         def _(o):
             sc_copy(o).wait_send()
 
-        for k in range(2):
-            for p in range(N):
-                @pl.when(feeds_join | (k == p % 2))
-                def _():
-                    v_copy(k, p).wait_send()
-
-    @pl.when(feeds_spread)
-    def _():
-        hop_copy(grad_own).wait_send()
+    @pl.when(s == TOP)
+    def _():
+        pair_copy(0).wait_send()
+        pair_copy(1).wait_send()
+        seed_copy().wait_send()
+        for o in range(4):
+            for h in range(2):
+                u_copy(h, o).wait_send()
 
         @pl.loop(0, N)
         def _(p):
-            wv_copy(p).wait_send()
+            mix_copy(p).wait_send()
+
+    @pl.when(second)
+    def _():
+        for items in u_forwards:
+            for item in items:
+                u_forward(*item).wait_send()
+
+    @pl.when((s >= 1) & (s < TOP))
+    def _():
+        gain_copy().wait_send()
+
+        for p in range(N):
+            @pl.when(feeds_join)
+            def _():
+                v_copy_both(p).wait_send()
+
+            @pl.when(feeds_spread)
+            def _():
+                v_copy_one(p).wait_send()
+
+    @pl.when(feeds_spread)
+    def _():
+        hop_copy(grad_own).wait_send()
+        stage_copy().wait_send()
 
     @pl.when(feeds_join)
     def _():
         for o in range(4):
             for h in range(2):
                 full_copy(h, o).wait_send()
-        for k in range(2):
-            whole_copy(k).wait_send()
+        for d in range(8):
+            whole_copy(d).wait_send()
 
     @pl.when(spreads)
     def _():
+        @pl.loop(1, N)
+        def _(o):
+            wv_copy(o).wait_send()
+
         for item in own_sends + sum(row_sends, []) + sum(col_sends, []):
             half_copy(*item).wait_send()
 
@@ -593,7 +827,7 @@
     dma = pltpu.SemaphoreType.DMA
     out = pl.pallas_call(
         chain_kernel,
-        out_shape=jax.ShapeDtypeStruct((16, ACT), F32),
+        out_shape=jax.ShapeDtypeStruct((6, 2, ACT), F32),
         in_specs=[hbm] * 11,
         out_specs=vmem,
         scratch_shapes=[
@@ -608,6 +842,7 @@
             pltpu.VMEM((8, 256), F32),
             pltpu.VMEM((8, 128), F32),
             pltpu.VMEM((512, 5120), BF16),
+            pltpu.VMEM((5120, 512), BF16),
             pltpu.VMEM((FEATS, 5120), BF16),
             pltpu.VMEM((1024, WIDE), BF16),
             pltpu.VMEM((1024, 5120), BF16),
@@ -616,32 +851,45 @@
             pltpu.VMEM((TOK, WIDE), BF16),
             pltpu.VMEM((TOK, WIDE), BF16),
             pltpu.VMEM((2, TOK, HD), BF16),
-            pltpu.VMEM((2, N, TOK, HD), BF16),
-            pltpu.VMEM((2, TOK, 1024), BF16),
-            pltpu.VMEM((TOK, HEADS_HERE * HD), F32),
+            pltpu.VMEM((N, 2, TOK, HD), BF16),
+            pltpu.VMEM((2 * TOK, 1024), BF16),
+            pltpu.VMEM((2 * TOK, HEADS_HERE * HD), F32),
             pltpu.VMEM((N, 8, 128), F32),
             pltpu.VMEM((TOK, 128), F32),
             pltpu.VMEM((8, 8, 256), F32),
             pltpu.VMEM((16, 256), BF16),
             pltpu.VMEM((N, 16, 256), BF16),
             pltpu.VMEM((TOK, HEADS_HERE * HD), BF16),
-            pltpu.VMEM((HEADS_HERE * HD, HD), BF16),
+            pltpu.VMEM((HEADS_HERE * HD, 2 * HD), BF16),
             pltpu.VMEM((128, 128), F32),
             pltpu.VMEM((2 * TOK, FEATS), F32),
             pltpu.VMEM((N, 16, ACT), BF16),
             pltpu.VMEM((N, 16, ACT), BF16),
-            dma((9,)),
+            dma((12,)),
             dma, dma,
             dma((N,)), dma((N,)),
             dma((2 * N,)), dma((2 * N,)),
             dma((N,)), dma((N,)),
             dma, dma((8,)),
             dma((N,)), dma((N,)),
-            dma((2 * N,)), dma((2 * N,)),
+            dma((N,)), dma((N,)),
             dma((3 * N,)), dma((2 * N,)),
             dma, dma,
+            dma((8,)), dma((8,)),
+            dma((N,)), dma((N,)),
+            pltpu.VMEM((16, 2560), BF16),
+            pltpu.VMEM((16, 2560), F32),
+            pltpu.VMEM((16, 2560), BF16),
+            pltpu.VMEM((N + 1, 16, 2560), BF16),
+            pltpu.VMEM((TOK, HD), BF16),
+            pltpu.VMEM((N, TOK, HD), BF16),
+            pltpu.VMEM((2, 2 * TOK, 2 * HD), BF16),
+            pltpu.VMEM((64, 5120), BF16),
+            dma, dma,
             dma((2,)), dma((2,)),
+            dma((40,)), dma((2 * N,)),
             dma((N,)), dma((N,)),
+            dma, dma,
         ],
         compiler_params=pltpu.CompilerParams(
             collective_id=0, has_side_effects=True, vmem_limit_bytes=63 * 2**20
@@ -652,7 +900,7 @@
         source_ids[0], source_values[0],
         out_weight[0], value_weight[0], decoder[0],
     )
-    return out.reshape(2, 8, ACT)[:, :6].transpose(1, 0, 2)[None]
+    return out[None]
 
 
 def solution(mesh):

time: 147 us -> 134 us (0.912)
  Pallas kernels: 146 us -> 133 us
    pallas_call x1, Pallas kernels: 146 us -> 133 us  [body(): pl.pallas_call(chain_kernel, out_shape=jax.ShapeDtypeStruct((6, 2, ACT),...]
where the time goes in v3:
time: 134 us
  Pallas kernels  133 us (99%)
    pallas_call x1, Pallas kernels, body(): pl.pallas_call(chain_kernel, out_shape=jax.ShapeDtypeStruct((6, 2, ACT),...  133 us

profile of v3, /device:TPU:0, one launch (start us, length us, event | category | flops | bytes accessed | tf_op | source)
XLA Modules:
  0.0 134.1 jit_solution(6748593701871175943)
XLA Ops:
  0.0 132.8 %chain.1 = f32[6,2,128]{2,1,0:T(2,128)} custom-call(bf16[40,16384]{1,0:T(8,128)(2,1)} %bitcast.10, f32[1,6]{1,0:T(1,128)} %scale_hbm.1, bf16[4,96,96]{2,1,0:T(8,128)(2,1)} %bitcast.12, f32[1,5120]{1,0:T(1,128)} %gain_hbm.1, s32[2]{0:T(128)} %want_hbm.1, s32[2]{0:T(128)} %tok_hbm.1, s32[96,128]{1,0:T(8,128)} %bitcast.13, f32[96,128]{1,0:T(8,128)} %bitcast.14, ...), custom_call_target="tpu_custom_call" | custom-call | tf_op jit(solution)/shard_map/chain/pallas_call | solution.py:828
  132.8 1.3 copy.13

commit v4 on v3

--- a/solution.py
+++ b/solution.py
@@ -48,11 +48,11 @@
     row = j // 4
     col = lax.rem(j, 4)
     below = s - 1
-    spreads = (s == 5) | (s == 4) | (s == 3) | (s == 1)
-    joins = (s == 2) | (s == 0)
+    spreads = (s == 5) | (s == 3) | (s == 1)
+    joins = (s == 4) | (s == 2) | (s == 0)
     second = s == TOP - 1
-    feeds_spread = (s == 6) | (s == 5) | (s == 4) | (s == 2)
-    feeds_join = (s == 3) | (s == 1)
+    feeds_spread = (s == 6) | (s == 4) | (s == 2)
+    feeds_join = (s == 5) | (s == 3) | (s == 1)
 
     def peer(o):
         return lax.rem(j + o, N)
@@ -189,10 +189,24 @@
     def half_rows(c, h):
         return wvf.at[pl.ds(pl.multiple_of(c * 64 + 32 * h, 32), 32)]
 
+    def quarter_rows(c, h, q):
+        return wvf.at[pl.ds(pl.multiple_of(c * 64 + 32 * h + 16 * q, 16), 16)]
+
+    def first_ring(h, o):
+        return at_col(o) if h else at_row(o)
+
+    def second_ring(h, o):
+        return at_row(o) if h else at_col(o)
+
+    def on_rings(h, o1, o2):
+        if h:
+            return lax.rem(row + o1, 4) * 4 + lax.rem(col + o2, 4)
+        return lax.rem(row + o2, 4) * 4 + lax.rem(col + o1, 4)
+
     def full_copy(h, o):
         return remote(
             wv_hbm.at[pl.ds(32 * h, 32)], half_rows(j, h),
-            wv_ssem.at[4 * h + o], fw_rsem.at[2 * j + h], below, at_col(o) if h else at_row(o),
+            wv_ssem.at[4 * h + o], fw_rsem.at[4 * j + 2 * h], below, first_ring(h, o),
         )
 
     def pair_rows(h, k):
@@ -234,7 +248,7 @@
 
     @pl.when(feeds_join)
     def _():
-        for o in (2, 1, 3, 0):
+        for o in (1, 3, 0):
             for h in range(2):
                 full_copy(h, o).start()
 
@@ -312,6 +326,7 @@
                 spot = 4 * k + h
                 slab = slab + jnp.where((place == spot) | (place == spot + 8), chosen, 0.0)
         mix_send[...] = (slab * sc_rows[...]).astype(BF16)
+        far_first(lambda p: mix_copy(p).start())
 
         @pl.loop(1, N)
         def _(o):
@@ -356,10 +371,6 @@
             for h in range(2):
                 u_copy(h, o).start()
 
-        @pl.loop(0, N)
-        def _(p):
-            mix_copy(p).start()
-
         token = lax.broadcasted_iota(jnp.int32, (TOK, WIDE), 0)
         for k in range(2):
             hit = token == tok_ref[k]
@@ -375,64 +386,100 @@
     def _():
         spread_scales()
 
-    forwards = []
-    for o in (0, 1, 3, 2):
-        forwards.append([(at_row(o), 0, at_col(q), 4 * o + q) for q in (2, 1, 3)])
-        forwards.append([(at_col(o), 1, at_row(q), 16 + 4 * o + q) for q in (2, 1, 3)])
-
-    def forward_copy(c, h, to, sem):
-        return remote(half_rows(c, h), half_rows(c, h), fw_ssem.at[sem], fw_rsem.at[2 * c + h], s, to)
-
-    @pl.when(joins)
-    def _():
-        for items in forwards:
-            c, h = items[0][0], items[0][1]
-            arrived(half_rows(c, h), fw_rsem.at[2 * c + h], fw_ssem.at[0])
-            for item in items:
-                forward_copy(*item).start()
-        arrived(gain_up, gain_rsem, gain_ssem)
-
-        @pl.loop(0, N)
-        def _(c):
-            @pl.when(c // 4 != row)
-            def _():
-                arrived(half_rows(c, 0), fw_rsem.at[2 * c], fw_ssem.at[0])
-
-            @pl.when(lax.rem(c, 4) != col)
-            def _():
-                arrived(half_rows(c, 1), fw_rsem.at[2 * c + 1], fw_ssem.at[0])
-
-        for items in forwards:
-            for item in items:
-                forward_copy(*item).wait_send()
-
-        @pl.loop(0, 64)
-        def _(i):
-            part = pl.ds(pl.multiple_of(i * 16, 16), 16)
-            wvf[part, :] = (wvf[part, :].astype(F32) * gain_up[...]).astype(BF16)
-
     @pl.when(s < TOP)
     def _():
         wo_copy.wait()
 
     dec_copy.wait()
 
-    @pl.when(spreads)
-    def _():
+    def transpose_weights():
         @pl.loop(0, 40)
         def _(i):
             part = pl.ds(pl.multiple_of(i * 128, 128), 128)
             wo_t[part, :] = wo[:, part].T
 
-    @pl.when(s == 2)
-    def _():
-        @pl.loop(0, 4)
+    sent = []
+
+    def pass_half(c, h, to):
+        sem = fw_ssem.at[len(sent)]
+        copy = remote(half_rows(c, h), half_rows(c, h), sem, fw_rsem.at[4 * c + 2 * h], s, to)
+        copy.start()
+        sent.append(copy)
+
+    def pass_quarter(c, h, q, to):
+        sem = fw_ssem.at[len(sent)]
+        part = quarter_rows(c, h, q)
+        copy = remote(part, part, sem, fw_rsem.at[4 * c + 2 * h + q], s, to)
+        copy.start()
+        sent.append(copy)
+
+    def half_here(c, h):
+        arrived(half_rows(c, h), fw_rsem.at[4 * c + 2 * h], fw_ssem.at[0])
+
+    def quarters_here(c, h):
+        for q in range(2):
+            arrived(quarter_rows(c, h, q), fw_rsem.at[4 * c + 2 * h + q], fw_ssem.at[0])
+
+    @pl.when(joins)
+    def _():
+        for o in (0, 1, 3):
+            for h in range(2):
+                c = on_rings(h, o, 0)
+                half_here(c, h)
+                if o == 3:
+                    pass_quarter(c, h, 0, first_ring(h, 1))
+                if o == 1:
+                    pass_quarter(c, h, 1, first_ring(h, 3))
+                pass_half(c, h, second_ring(h, 1))
+                pass_half(c, h, second_ring(h, 3))
+        for h in range(2):
+            c = on_rings(h, 2, 0)
+            quarters_here(c, h)
+            pass_half(c, h, second_ring(h, 1))
+            pass_half(c, h, second_ring(h, 3))
+        arrived(gain_up, gain_rsem, gain_ssem)
+        for step, o in enumerate((0, 1, 3, 2)):
+            @pl.when(s >= 2)
+            def _():
+                @pl.loop(10 * step, 10 * step + 10)
+                def _(i):
+                    part = pl.ds(pl.multiple_of(i * 128, 128), 128)
+                    scaled = wo[:, part].astype(F32) * gain_up[:, part]
+                    wo_t[part, :] = scaled.T.astype(BF16)
+
+            for h in range(2):
+                c = on_rings(h, o, 3)
+                half_here(c, h)
+                pass_quarter(c, h, 0, second_ring(h, 1))
+                c = on_rings(h, o, 1)
+                half_here(c, h)
+                pass_quarter(c, h, 1, second_ring(h, 3))
+        for o in (0, 1, 3, 2):
+            for h in range(2):
+                quarters_here(on_rings(h, o, 2), h)
+        for copy in sent:
+            copy.wait_send()
+
+        @pl.when(s == 0)
+        def _():
+            @pl.loop(0, 64)
+            def _(i):
+                part = pl.ds(pl.multiple_of(i * 16, 16), 16)
+                wvf[part, :] = (wvf[part, :].astype(F32) * gain_up[...]).astype(BF16)
+
+    @pl.when(spreads)
+    def _():
+        transpose_weights()
+
+    @pl.when((s == 4) | (s == 2))
+    def _():
+        @pl.loop(0, 2)
         def _(i):
-            part = pl.ds(pl.multiple_of(i * 256, 256), 256)
-            total = jnp.zeros((256, HEADS_HERE * HD), F32)
+            part = pl.ds(pl.multiple_of(i * 512, 512), 512)
+            total = jnp.zeros((512, HEADS_HERE * HD), F32)
             for d in range(8):
                 cols = slice(d * WIDE, (d + 1) * WIDE)
-                total += nt_dot(wvf[part, cols], wo[:, cols])
+                total += jnp.dot(wvf[part, cols], wo_t[cols, :], preferred_element_type=F32)
             joint[part, 0 : HEADS_HERE * HD] = total.astype(BF16)
 
     @pl.when(s == 0)
@@ -515,10 +562,6 @@
         for item in own_sends:
             half_copy(*item).start()
 
-        @pl.when(feeds_spread)
-        def _():
-            hop_copy(grad.at[j]).start()
-
     def forward(k):
         for items in row_sends:
             c = items[0][0]
@@ -582,10 +625,7 @@
         def take_chunks(d):
             wait_chunk(2 * d)
             wait_chunk(2 * d + 1)
-
-            @pl.when(feeds_join)
-            def _():
-                whole_copy(d).start()
+            whole_copy(d).start()
 
         send_values(head_grad_of(
             take_chunks,
@@ -605,6 +645,7 @@
 
     @pl.when(second)
     def _():
+        transpose_weights()
         for items in u_forwards:
             c, h = items[0][0], items[0][1]
             arrived(u_half(c, h), u_rsem.at[2 * c + h], u_ssem.at[0])
@@ -640,8 +681,8 @@
 
         half = 2560
         flat = u_recv[...].reshape(16 * (N + 1), half)
-        low = nt_dot(flat, wo[:, 0:half])
-        high = nt_dot(flat, wo[:, half:])
+        low = jnp.dot(flat, wo_t[0:half, :], preferred_element_type=F32)
+        high = jnp.dot(flat, wo_t[half:, :], preferred_element_type=F32)
         total = jnp.dot(mix[0], low[0:256].astype(BF16), preferred_element_type=F32)
         total += jnp.dot(mix[1], high[0:256].astype(BF16), preferred_element_type=F32)
         token = lax.broadcasted_iota(jnp.int32, (TOK, HEADS_HERE * HD), 0)
@@ -664,26 +705,27 @@
                 ).astype(BF16)
         hop_copy(grad.at[j]).start()
 
-    @pl.when(s == 2)
+    @pl.when((s == 4) | (s == 2))
     def _():
         base[...] = head_grad_of(whole_arrived, lambda both, part: nt_dot(both, wo[:, part]))
         wait_values()
         for k in range(2):
             v_full[k * TOK : (k + 1) * TOK, :] = value_grad(k)
+        mixed = jnp.dot(
+            v_full[pl.ds(pl.multiple_of(my_k * TOK, TOK), TOK), :], wvf[:, own_cols],
+            preferred_element_type=F32,
+        )
+        grad_own[...] = (grad[j].astype(F32) + mixed * gain_up[:, own_cols]).astype(BF16)
+        hop_copy(grad_own).start()
         total = base[...] + jnp.dot(
             v_full[...], joint[:, 0 : HEADS_HERE * HD], preferred_element_type=F32
         )
         send_values(total.astype(BF16))
-        mixed = jnp.dot(
-            v_full[pl.ds(pl.multiple_of(my_k * TOK, TOK), TOK), :], wvf[:, own_cols],
-            preferred_element_type=F32,
-        )
-        grad_own[...] = (grad[j].astype(F32) + mixed).astype(BF16)
-        hop_copy(grad_own).start()
         for d in range(8):
             mixed = jnp.dot(
                 v_full[...], wvf[:, d * WIDE : (d + 1) * WIDE], preferred_element_type=F32
             )
+            mixed = mixed * gain_up[:, d * WIDE : (d + 1) * WIDE]
             for k in range(2):
                 grad[2 * d + k] = (
                     grad[2 * d + k].astype(F32) + mixed[k * TOK : (k + 1) * TOK]
@@ -802,7 +844,7 @@
 
     @pl.when(feeds_join)
     def _():
-        for o in range(4):
+        for o in (0, 1, 3):
             for h in range(2):
                 full_copy(h, o).wait_send()
         for d in range(8):
@@ -868,7 +910,7 @@
             dma((12,)),
             dma, dma,
             dma((N,)), dma((N,)),
-            dma((2 * N,)), dma((2 * N,)),
+            dma((3 * N,)), dma((4 * N,)),
             dma((N,)), dma((N,)),
             dma, dma((8,)),
             dma((N,)), dma((N,)),

time: 134 us -> 131 us (0.978)
  Pallas kernels: 133 us -> 129 us
    pallas_call x1, Pallas kernels: 133 us -> 129 us  [body(): pl.pallas_call(chain_kernel, out_shape=jax.ShapeDtypeStruct((6, 2, ACT),...]
where the time goes in v4:
time: 131 us
  Pallas kernels  129 us (98%)
    pallas_call x1, Pallas kernels, body(): pl.pallas_call(chain_kernel, out_shape=jax.ShapeDtypeStruct((6, 2, ACT),...  129 us

profile of v4, /device:TPU:0, one launch (start us, length us, event | category | flops | bytes accessed | tf_op | source)
XLA Modules:
  0.0 130.8 jit_solution(8008661095351027587)
XLA Ops:
  0.0 129.5 %chain.1 = f32[6,2,128]{2,1,0:T(2,128)} custom-call(bf16[40,16384]{1,0:T(8,128)(2,1)} %bitcast.10, f32[1,6]{1,0:T(1,128)} %scale_hbm.1, bf16[4,96,96]{2,1,0:T(8,128)(2,1)} %bitcast.12, f32[1,5120]{1,0:T(1,128)} %gain_hbm.1, s32[2]{0:T(128)} %want_hbm.1, s32[2]{0:T(128)} %tok_hbm.1, s32[96,128]{1,0:T(8,128)} %bitcast.13, f32[96,128]{1,0:T(8,128)} %bitcast.14, ...), custom_call_target="tpu_custom_call" | custom-call | tf_op jit(solution)/shard_map/chain/pallas_call | solution.py:870
  129.5 1.3 copy.13

commit v5 on v4

--- a/solution.py
+++ b/solution.py
@@ -50,8 +50,9 @@
     below = s - 1
     spreads = (s == 5) | (s == 3) | (s == 1)
     joins = (s == 4) | (s == 2) | (s == 0)
-    second = s == TOP - 1
-    feeds_spread = (s == 6) | (s == 4) | (s == 2)
+    second_index = TOP - 1
+    second = s == second_index
+    feeds_spread = (s == 4) | (s == 2)
     feeds_join = (s == 5) | (s == 3) | (s == 1)
 
     def peer(o):
@@ -184,6 +185,20 @@
         p = peer(o)
         return remote(columns_of(p), wvs.at[own_rows], wv_ssem.at[o], wv_rsem.at[j], s, p)
 
+    def column_copy(h, o):
+        p = peer(o)
+        cols = pl.ds(pl.multiple_of((p // 2) * WIDE, 128), WIDE)
+        return remote(
+            wv_hbm.at[pl.ds(32 * h, 32), cols], half_columns(h, j),
+            wv_ssem.at[N * h + o], wv_rsem.at[N * h + j], s, p,
+        )
+
+    def half_columns(h, p):
+        return wvs.at[pl.ds(pl.multiple_of(p * 64 + 32 * h, 32), 32)]
+
+    straight_columns = pltpu.make_async_copy(
+        wv_hbm.at[:, pl.ds(pl.multiple_of(my_d * WIDE, 128), WIDE)], wvs.at[own_rows], local_sem.at[11]
+    )
     own_columns = pltpu.make_async_copy(columns_of(j), wvs.at[own_rows], local_sem.at[11])
 
     def half_rows(c, h):
@@ -226,9 +241,12 @@
     @pl.when(s == TOP)
     def _():
         own_wv.start()
+
+    @pl.when(s >= second_index)
+    def _():
         own_gain.start()
 
-    @pl.when((s >= 1) & (s < TOP))
+    @pl.when((s >= 1) & (s < second_index))
     def _():
         gain_copy().start()
 
@@ -265,7 +283,7 @@
         pad[0:TOK, 0:TOK] = weights / jnp.sum(weights, axis=-1, keepdims=True)
         pat[:, h * HD : (h + 1) * HD] = pad[...].T[0:TOK, :].astype(BF16)
 
-    @pl.when(spreads)
+    @pl.when((s == 3) | (s == 1))
     def _():
         arrived(wv_stage, stage_rsem, stage_ssem)
         own_columns.start()
@@ -299,6 +317,9 @@
 
     def hop_copy(src):
         return remote(src, grad_base, hop_ssem, hop_rsem, below, j)
+
+    def last_copy():
+        return remote(grad_own, grad.at[j], hop_ssem, hop_rsem, below, j)
 
     @pl.when(s == TOP)
     def _():
@@ -496,7 +517,7 @@
     def wait_values():
         @pl.loop(0, N)
         def _(p):
-            @pl.when(spreads)
+            @pl.when(spreads | (second & (p != j)))
             def _():
                 arrived(v_recv.at[p, 0], v_rsem.at[p], v_ssem.at[0])
 
@@ -516,6 +537,11 @@
 
     def v_copy_one(p):
         return remote(v_send.at[lax.rem(p, 2)], v_recv.at[j, 0], v_ssem.at[p], v_rsem.at[j], below, p)
+
+    def v_copy_here(p):
+        return remote(
+            v_send.at[lax.rem(p, 2)], v_recv.at[j, 0], v_ssem.at[p], v_rsem.at[j], s, p
+        )
 
     def send_values(head_grad):
         for k in range(2):
@@ -534,6 +560,11 @@
         @pl.when(feeds_spread)
         def _():
             far_first(lambda p: v_copy_one(p).start())
+
+        @pl.when(second)
+        def _():
+            far_first_peers(lambda p: v_copy_here(p).start())
+            v_recv[j, 0] = v_send[my_k]
 
     def half_copy(c, h, to, sem):
         part = grad.at[c, pl.ds(48 * h, 48)]
@@ -555,10 +586,20 @@
 
     own_cols = pl.ds(pl.multiple_of(my_d * WIDE, 128), WIDE)
 
-    def make_chunk():
+    def next_chunk(chunk):
         wait_values()
         mixed = jnp.dot(value_grad(0), wvs[...], preferred_element_type=F32)
-        grad[j] = (grad_base[...].astype(F32) + mixed * gain_up[:, own_cols]).astype(BF16)
+        return (chunk[...].astype(F32) + mixed * gain_up[:, own_cols]).astype(BF16)
+
+    def make_chunk():
+        @pl.when(s == 5)
+        def _():
+            arrived(grad.at[j], hop_rsem, hop_ssem)
+
+        @pl.when(s < 5)
+        def _():
+            grad[j] = next_chunk(grad_base)
+
         for item in own_sends:
             half_copy(*item).start()
 
@@ -603,7 +644,7 @@
             total += dot(both, slice(d * WIDE, (d + 1) * WIDE))
         return total
 
-    @pl.when(spreads)
+    @pl.when((s == 3) | (s == 1))
     def _():
         arrived(gain_up, gain_rsem, gain_ssem)
         own_columns.wait()
@@ -645,18 +686,28 @@
 
     @pl.when(second)
     def _():
+        straight_columns.start()
         transpose_weights()
+        arrived(u_recv.at[N], seed_rsem, seed_ssem)
+
+        @pl.loop(1, N)
+        def _(o):
+            column_copy(0, o).start()
+
         for items in u_forwards:
             c, h = items[0][0], items[0][1]
             arrived(u_half(c, h), u_rsem.at[2 * c + h], u_ssem.at[0])
             for item in items:
                 u_forward(*item).start()
 
+        @pl.loop(1, N)
+        def _(o):
+            column_copy(1, o).start()
+
         @pl.loop(0, N)
         def _(p):
             arrived(mix_recv.at[p], mix_rsem.at[p], mix_ssem.at[0])
 
-        arrived(u_recv.at[N], seed_rsem, seed_ssem)
         kind = lax.broadcasted_iota(jnp.int32, (TOK, HD), 1) & 15
         for t in range(2):
             tile = jnp.zeros((TOK, HD), F32)
@@ -703,7 +754,17 @@
                 grad[2 * d + k] = (
                     mixed[k * TOK : (k + 1) * TOK] + jnp.where(token == tok_ref[k], one, 0.0)
                 ).astype(BF16)
-        hop_copy(grad.at[j]).start()
+        own_gain.wait()
+        straight_columns.wait()
+
+        @pl.loop(1, N)
+        def _(o):
+            p = peer(o)
+            for h in range(2):
+                arrived(half_columns(h, p), wv_rsem.at[N * h + p], wv_ssem.at[0])
+
+        grad_own[...] = next_chunk(grad.at[j])
+        last_copy().start()
 
     @pl.when((s == 4) | (s == 2))
     def _():
@@ -820,11 +881,19 @@
 
     @pl.when(second)
     def _():
+        last_copy().wait_send()
+        far_first_peers(lambda p: v_copy_here(p).wait_send())
+
+        @pl.loop(1, N)
+        def _(o):
+            for h in range(2):
+                column_copy(h, o).wait_send()
+
         for items in u_forwards:
             for item in items:
                 u_forward(*item).wait_send()
 
-    @pl.when((s >= 1) & (s < TOP))
+    @pl.when((s >= 1) & (s < second_index))
     def _():
         gain_copy().wait_send()
 
@@ -850,12 +919,14 @@
         for d in range(8):
             whole_copy(d).wait_send()
 
+    @pl.when((s == 3) | (s == 1))
+    def _():
+        @pl.loop(1, N)
+        def _(o):
+            wv_copy(o).wait_send()
+
     @pl.when(spreads)
     def _():
-        @pl.loop(1, N)
-        def _(o):
-            wv_copy(o).wait_send()
-
         for item in own_sends + sum(row_sends, []) + sum(col_sends, []):
             half_copy(*item).wait_send()
 
@@ -909,7 +980,7 @@
             pltpu.VMEM((N, 16, ACT), BF16),
             dma((12,)),
             dma, dma,
-            dma((N,)), dma((N,)),
+            dma((2 * N,)), dma((2 * N,)),
             dma((3 * N,)), dma((4 * N,)),
             dma((N,)), dma((N,)),
             dma, dma((8,)),

time: 131 us -> 129 us (0.985)
  Pallas kernels: 129 us -> 127 us
    pallas_call x1, Pallas kernels: 129 us -> 127 us  [body(): pl.pallas_call(chain_kernel, out_shape=jax.ShapeDtypeStruct((6, 2, ACT),...]
where the time goes in v5:
time: 129 us
  Pallas kernels  127 us (98%)
  local copies, waits for them, and re-layouts  1.29 us (1%)
    pallas_call x1, Pallas kernels, body(): pl.pallas_call(chain_kernel, out_shape=jax.ShapeDtypeStruct((6, 2, ACT),...  127 us

profile of v5, /device:TPU:0, one launch (start us, length us, event | category | flops | bytes accessed | tf_op | source)
XLA Modules:
  0.0 128.7 jit_solution(2971334755201744454)
XLA Ops:
  0.0 127.5 %chain.1 = f32[6,2,128]{2,1,0:T(2,128)} custom-call(bf16[40,16384]{1,0:T(8,128)(2,1)} %bitcast.10, f32[1,6]{1,0:T(1,128)} %scale_hbm.1, bf16[4,96,96]{2,1,0:T(8,128)(2,1)} %bitcast.12, f32[1,5120]{1,0:T(1,128)} %gain_hbm.1, s32[2]{0:T(128)} %want_hbm.1, s32[2]{0:T(128)} %tok_hbm.1, s32[96,128]{1,0:T(8,128)} %bitcast.13, f32[96,128]{1,0:T(8,128)} %bitcast.14, ...), custom_call_target="tpu_custom_call" | custom-call | tf_op jit(solution)/shard_map/chain/pallas_call | solution.py:941
  127.5 1.3 copy.13

commit v6 on v5

--- a/solution.py
+++ b/solution.py
@@ -292,6 +292,12 @@
         def _(o):
             wv_copy(o).start()
 
+    def transpose_weights():
+        @pl.loop(0, 40)
+        def _(i):
+            part = pl.ds(pl.multiple_of(i * 128, 128), 128)
+            wo_t[part, :] = wo[:, part].T
+
     def u_copy(h, o):
         part = u_recv.at[j, :, pl.ds(1280 * h, 1280)]
         return remote(
@@ -348,6 +354,8 @@
                 slab = slab + jnp.where((place == spot) | (place == spot + 8), chosen, 0.0)
         mix_send[...] = (slab * sc_rows[...]).astype(BF16)
         far_first(lambda p: mix_copy(p).start())
+        wo_copy.wait()
+        transpose_weights()
 
         @pl.loop(1, N)
         def _(o):
@@ -370,10 +378,9 @@
                 seeds[k : k + 1, cols] = low.astype(BF16)
                 seeds[8 + k : 9 + k, cols] = high.astype(BF16)
         seed_copy().start()
-        wo_copy.wait()
         half = 2560
-        low = nt_dot(seeds[...], wo[:, 0:half])
-        high = nt_dot(seeds[...], wo[:, half:])
+        low = jnp.dot(seeds[...], wo_t[0:half, :], preferred_element_type=F32)
+        high = jnp.dot(seeds[...], wo_t[half:, :], preferred_element_type=F32)
         rows = low[0:2] + high[8:10]
         parts = [
             rows[k : k + 1, h * HD : (h + 1) * HD] for k in range(2) for h in range(HEADS_HERE)
@@ -413,11 +420,6 @@
 
     dec_copy.wait()
 
-    def transpose_weights():
-        @pl.loop(0, 40)
-        def _(i):
-            part = pl.ds(pl.multiple_of(i * 128, 128), 128)
-            wo_t[part, :] = wo[:, part].T
 
     sent = []
 
@@ -514,16 +516,16 @@
                 total += nt_dot(wvf[part, cols], dec[:, cols])
             joint[part, :] = total.astype(BF16)
 
+    def wait_one_target(first):
+        @pl.loop(first, N)
+        def _(o):
+            p = peer(o)
+            arrived(v_recv.at[p, 0], v_rsem.at[p], v_ssem.at[0])
+
     def wait_values():
         @pl.loop(0, N)
         def _(p):
-            @pl.when(spreads | (second & (p != j)))
-            def _():
-                arrived(v_recv.at[p, 0], v_rsem.at[p], v_ssem.at[0])
-
-            @pl.when(joins)
-            def _():
-                arrived(v_recv.at[p], v_rsem.at[p], v_ssem.at[0])
+            arrived(v_recv.at[p], v_rsem.at[p], v_ssem.at[0])
 
     def value_grad(k):
         pieces = []
@@ -586,8 +588,8 @@
 
     own_cols = pl.ds(pl.multiple_of(my_d * WIDE, 128), WIDE)
 
-    def next_chunk(chunk):
-        wait_values()
+    def next_chunk(chunk, first):
+        wait_one_target(first)
         mixed = jnp.dot(value_grad(0), wvs[...], preferred_element_type=F32)
         return (chunk[...].astype(F32) + mixed * gain_up[:, own_cols]).astype(BF16)
 
@@ -598,27 +600,16 @@
 
         @pl.when(s < 5)
         def _():
-            grad[j] = next_chunk(grad_base)
+            grad[j] = next_chunk(grad_base, 0)
 
         for item in own_sends:
             half_copy(*item).start()
 
-    def forward(k):
-        for items in row_sends:
-            c = items[0][0]
-
-            @pl.when(lax.rem(c, 2) == k)
-            def _():
-                half_arrived(c, 0)
-                for item in items:
-                    half_copy(*item).start()
-
-        @pl.when(my_k == k)
-        def _():
-            for items in col_sends:
-                half_arrived(items[0][0], 1)
-                for item in items:
-                    half_copy(*item).start()
+    def forward():
+        for items in sum(zip(row_sends, col_sends), ()):
+            half_arrived(*items[0][:2])
+            for item in items:
+                half_copy(*item).start()
 
     def wait_chunk(c):
         @pl.when(c // 4 != row)
@@ -660,8 +651,7 @@
     @pl.when(spreads)
     def _():
         make_chunk()
-        forward(0)
-        forward(1)
+        forward()
 
         def take_chunks(d):
             wait_chunk(2 * d)
@@ -763,7 +753,7 @@
             for h in range(2):
                 arrived(half_columns(h, p), wv_rsem.at[N * h + p], wv_ssem.at[0])
 
-        grad_own[...] = next_chunk(grad.at[j])
+        grad_own[...] = next_chunk(grad.at[j], 1)
         last_copy().start()
 
     @pl.when((s == 4) | (s == 2))

time: 129 us -> 129 us (level)
  no operation moved by 1% of the time
where the time goes in v6:
time: 129 us
  Pallas kernels  127 us (98%)
  local copies, waits for them, and re-layouts  1.29 us (1%)
    pallas_call x1, Pallas kernels, body(): pl.pallas_call(chain_kernel, out_shape=jax.ShapeDtypeStruct((6, 2, ACT),...  127 us

profile of v6, /device:TPU:0, one launch (start us, length us, event | category | flops | bytes accessed | tf_op | source)
XLA Modules:
  0.0 128.7 jit_solution(16807353705159425550)
XLA Ops:
  0.0 127.4 %chain.1 = f32[6,2,128]{2,1,0:T(2,128)} custom-call(bf16[40,16384]{1,0:T(8,128)(2,1)} %bitcast.10, f32[1,6]{1,0:T(1,128)} %scale_hbm.1, bf16[4,96,96]{2,1,0:T(8,128)(2,1)} %bitcast.12, f32[1,5120]{1,0:T(1,128)} %gain_hbm.1, s32[2]{0:T(128)} %want_hbm.1, s32[2]{0:T(128)} %tok_hbm.1, s32[96,128]{1,0:T(8,128)} %bitcast.13, f32[96,128]{1,0:T(8,128)} %bitcast.14, ...), custom_call_target="tpu_custom_call" | custom-call | tf_op jit(solution)/shard_map/chain/pallas_call | solution.py:931
  127.4 1.3 copy.13
